TPU v7x, 128 devices: a whole 4x4x4 slice. The times are simulated.
128 devices in a mesh: tm: 8 (over x, core), space: 16 (over y, z).
Axes of the slice: x: 4, y: 4, z: 4, core: 2. Of those that a mesh axis runs over, the one named last changes fastest.
Arguments:
- activations: bfloat16 [16, 64, 192, 128], P('tm', 'space')
- weight_one: bfloat16 [5184, 192], replicated, may hold values from -0.078125 to 0.078125
- weight_two: bfloat16 [5184, 192], replicated, may hold values from -0.078125 to 0.078125
- gain_one: float32 [192], replicated, may hold values from 0.1 to 1.9
- bias_one: float32 [192], replicated, may hold values from -3 to 3
- gain_two: float32 [192], replicated, may hold values from 0.1 to 1.9
- bias_two: float32 [192], replicated, may hold values from -3 to 3
- cotangent: bfloat16 [16, 64, 192, 128], P('tm', 'space'), may hold values from -6 to 6
- clip_lengths: int32 [4], replicated, may hold values from 1 to 8, as said below
Outputs:
- decoded: bfloat16 [16, 64, 192, 128], P('tm', 'space')
- input_grad: bfloat16 [16, 64, 192, 128], P('tm', 'space')
- weight_grad_one: float32 [5184, 192], P('space')
- weight_grad_two: float32 [5184, 192], P('space')
Inputs may be any that keep to these rules, and one draw needn't show every extreme that they name: `clip_lengths`: the 4 clip lengths sum to 16; the last clip has exactly 8 frames and no clip is longer.
All inputs are finite; a program needn't handle non-finite values.
Results may differ from a plain program's by a relative error of at most 0.0056.
Values may be sent and summed in bfloat16 or wider, within the bound.
No kernel may reach another device: no remote copies, remote signals or barrier semaphores. Data moves between devices by JAX's collectives and lax.ppermute only.
A program may use at most 128 MiB of HBM per device.

v0:
```python
import jax
import jax.numpy as jnp
from jax import lax
from jax.sharding import PartitionSpec as P

GROUPS = 32


NORM_EPSILON = 1e-05


def from_behind(block, axis, distance):
    devices = range(lax.axis_size(axis))
    route = [(i - distance, i) for i in devices if i - distance in devices]
    return lax.ppermute(block, axis, route)


def padded(cells, sides, width):
    for axis, dim in sides:
        count = lax.axis_size(axis)
        ends = count - 1
        head = lax.slice_in_dim(cells, 0, width, axis=dim)
        tail = lax.slice_in_dim(cells, cells.shape[dim] - width, cells.shape[dim], axis=dim)
        cells = jnp.concatenate(
            [
                lax.ppermute(tail, axis, [(i, (i + 1) % count) for i in range(ends)]),
                cells,
                lax.ppermute(head, axis, [((i + 1) % count, i) for i in range(ends)]),
            ],
            axis=dim,
        )
    return cells


def keep_table(first_frame, frame_count, clip_ends):
    frame_ids = first_frame + jnp.arange(frame_count, dtype=jnp.int32)
    own_clip = jnp.sum((frame_ids[:, None] >= clip_ends[None, :]).astype(jnp.int32), axis=1)
    lagged = [jnp.ones((frame_count,), jnp.float32)]
    for lag_size in (1, 2):
        shifted_ids = frame_ids - lag_size
        before_clip = jnp.sum(
            (shifted_ids[:, None] >= clip_ends[None, :]).astype(jnp.int32), axis=1
        )
        allowed = (shifted_ids >= 0) & (before_clip == own_clip)
        lagged.append(allowed.astype(jnp.float32))
    return jnp.stack(lagged)


def spatial_conv(source, kernel):
    return lax.conv_general_dilated(
        source,
        kernel,
        (1, 1),
        ((0, 0), (1, 1)),
        dimension_numbers=("NHCW", "HWIO", "NHCW"),
        preferred_element_type=jnp.float32,
    )


def extend_back(active):
    cached = from_behind(active[-2:], "tm", 1)
    joined = jnp.concatenate([cached, active], axis=0)
    return padded(joined, (("space", 1),), 1)


def extend_ahead(gradient):
    later_part = from_behind(gradient[:2], "tm", -1)
    joined = jnp.concatenate([gradient, later_part], axis=0)
    return padded(joined, (("space", 1),), 1)


def conv_forward(extended, kernel, keep_back, frame_count):
    summed = None
    for tap_index in range(3):
        lag_size = 2 - tap_index
        part_sum = spatial_conv(extended[tap_index : tap_index + frame_count], kernel[tap_index])
        part_sum = part_sum * keep_back[lag_size][:, None, None, None]
        summed = part_sum if summed is None else summed + part_sum
    return summed


def conv_adjoint(ahead, kernel, keep_ahead, frame_count):
    summed = None
    for tap_index in range(3):
        lag_size = 2 - tap_index
        factor = keep_ahead[lag_size][lag_size : lag_size + frame_count].astype(jnp.bfloat16)
        source = ahead[lag_size : lag_size + frame_count] * factor[:, None, None, None]
        flipped = jnp.swapaxes(jnp.flip(kernel[tap_index], (0, 1)), 2, 3)
        part_sum = spatial_conv(source, flipped)
        summed = part_sum if summed is None else summed + part_sum
    return summed


def weight_gradient(extended, gradient, keep_back, frame_count):
    padded_cols = jnp.pad(extended, ((0, 0), (0, 0), (0, 0), (1, 1)))
    height = gradient.shape[1]
    columns = gradient.shape[3]
    blocks = []
    for tap_index in range(3):
        lag_size = 2 - tap_index
        masked = gradient * keep_back[lag_size].astype(jnp.bfloat16)[:, None, None, None]
        for row_tap in range(3):
            for col_tap in range(3):
                window_piece = padded_cols[
                    tap_index : tap_index + frame_count,
                    row_tap : row_tap + height,
                    :,
                    col_tap : col_tap + columns,
                ]
                blocks.append(
                    jnp.einsum(
                        "thcw,thow->co", window_piece, masked, preferred_element_type=jnp.float32
                    )
                )
    return jnp.concatenate(blocks, axis=0)


def norm_forward(tensor, gain, bias):
    frame_count, height, channels, columns = tensor.shape
    grouped = tensor.reshape(frame_count, height, GROUPS, channels // GROUPS, columns)
    cell_count = height * lax.axis_size("space") * (channels // GROUPS) * columns
    mean_value = lax.psum(jnp.sum(grouped, axis=(1, 3, 4)), "space") / cell_count
    centered = grouped - mean_value[:, None, :, None, None]
    variance = lax.psum(jnp.sum(centered * centered, axis=(1, 3, 4)), "space") / cell_count
    inverse = lax.rsqrt(variance + NORM_EPSILON)[:, None, :, None, None]
    normalized = (centered * inverse).reshape(tensor.shape)
    pre_act = normalized * gain[None, None, :, None] + bias[None, None, :, None]
    return (normalized, inverse, pre_act)


def norm_adjoint(upstream, normalized, inverse, pre_act, gain):
    frame_count, height, channels, columns = upstream.shape
    group_shape = (frame_count, height, GROUPS, channels // GROUPS, columns)
    cell_count = height * lax.axis_size("space") * (channels // GROUPS) * columns
    sigmoid_value = jax.nn.sigmoid(pre_act)
    grad_pre = upstream * sigmoid_value * (1.0 + pre_act * (1.0 - sigmoid_value))
    grad_norm = (grad_pre * gain[None, None, :, None]).reshape(group_shape)
    norm_grouped = normalized.reshape(group_shape)
    plain_sum, weighted_sum = lax.psum(
        (jnp.sum(grad_norm, axis=(1, 3, 4)), jnp.sum(grad_norm * norm_grouped, axis=(1, 3, 4))),
        "space",
    )
    result = inverse * (
        grad_norm
        - (plain_sum / cell_count)[:, None, :, None, None]
        - norm_grouped * (weighted_sum / cell_count)[:, None, :, None, None]
    )
    return result.reshape(upstream.shape)


def shards(
    activations,
    weight_one,
    weight_two,
    gain_one,
    bias_one,
    gain_two,
    bias_two,
    cotangent,
    clip_lengths,
):
    frame_count, height, channels, columns = activations.shape
    clip_ends = jnp.cumsum(clip_lengths)
    first_frame = lax.axis_index("tm") * frame_count
    keep_back = keep_table(first_frame, frame_count, clip_ends)
    keep_ahead = keep_table(first_frame, frame_count + 2, clip_ends)
    kernel_one = weight_one.reshape(3, 3, 3, channels, channels)
    kernel_two = weight_two.reshape(3, 3, 3, channels, channels)
    inputs = activations.astype(jnp.float32)
    normalized_one, inverse_one, pre_one = norm_forward(inputs, gain_one, bias_one)
    active_one = jax.nn.silu(pre_one).astype(jnp.bfloat16)
    extended_one = extend_back(active_one)
    conv_one = conv_forward(extended_one, kernel_one, keep_back, frame_count)
    normalized_two, inverse_two, pre_two = norm_forward(conv_one, gain_two, bias_two)
    active_two = jax.nn.silu(pre_two).astype(jnp.bfloat16)
    extended_two = extend_back(active_two)
    conv_two = conv_forward(extended_two, kernel_two, keep_back, frame_count)
    decoded = (inputs + conv_two).astype(jnp.bfloat16)
    ahead_two = extend_ahead(cotangent)
    grad_active_two = conv_adjoint(ahead_two, kernel_two, keep_ahead, frame_count)
    local_grad_two = weight_gradient(extended_two, cotangent, keep_back, frame_count)
    grad_conv_one = norm_adjoint(
        grad_active_two, normalized_two, inverse_two, pre_two, gain_two
    ).astype(jnp.bfloat16)
    ahead_one = extend_ahead(grad_conv_one)
    grad_active_one = conv_adjoint(ahead_one, kernel_one, keep_ahead, frame_count)
    local_grad_one = weight_gradient(extended_one, grad_conv_one, keep_back, frame_count)
    grad_inputs = norm_adjoint(grad_active_one, normalized_one, inverse_one, pre_one, gain_one)
    input_grad = (cotangent.astype(jnp.float32) + grad_inputs).astype(jnp.bfloat16)
    total_cells = frame_count * lax.axis_size("tm") * height * lax.axis_size("space") * columns
    grad_scale = 1.0 / jnp.sqrt(jnp.float32(total_cells))
    summed_one, summed_two = lax.psum((local_grad_one, local_grad_two), "tm")
    share_one, share_two = (
        lax.psum_scatter(summed_one, "space", scatter_dimension=0, tiled=True),
        lax.psum_scatter(summed_two, "space", scatter_dimension=0, tiled=True),
    )
    return (decoded, input_grad, share_one * grad_scale, share_two * grad_scale)


def solution(mesh):
    placed = (
        P("tm", "space", None, None),
        P(),
        P(),
        P(),
        P(),
        P(),
        P(),
        P("tm", "space", None, None),
        P(),
    )
    return jax.shard_map(
        shards,
        mesh=mesh,
        in_specs=placed,
        out_specs=(
            P("tm", "space", None, None),
            P("tm", "space", None, None),
            P("space", None),
            P("space", None),
        ),
        check_vma=False,
    )
```

profile of v0, /device:TPU:1, one launch (start us, length us, event | category | flops | bytes accessed | tf_op | source)
XLA Modules:
  0.0 613.3 jit_solution(10263234048286101732)
XLA Ops:
  8.6 35.6 %psum.70 = f32[2,32]{1,0:T(2,128)S(1)} all-reduce(f32[2,32]{1,0:T(2,128)S(1)} %reduce_sum.148), channel_id=1, replica_groups=mesh['tm'=8,'space'=16] {'space'}, use_global_device_ids=true, to_apply=%region_2.3 | all-reduce | flops 64 | bytes 512 | tf_op jit(solution)/shard_map/psum | solution.py:122
  45.9 28.5 %psum.71 = f32[2,32]{1,0:T(2,128)S(1)} all-reduce(f32[2,32]{1,0:T(2,128)S(1)} %reduce_sum.154), channel_id=1, replica_groups=mesh['tm'=8,'space'=16] {'space'}, use_global_device_ids=true, to_apply=%region_5.6 | all-reduce | flops 64 | bytes 512 | tf_op jit(solution)/shard_map/psum | solution.py:124
  75.7 17.8 %collective-permute-start = (bf16[2,4,192,128]{3,2,0,1:T(8,128)(2,1)S(1)}, bf16[2,4,192,128]{3,2,0,1:T(8,128)(2,1)S(1)}, u32[]{:S(2)}, u32[]{:S(2)}) collective-permute-start(bf16[2,4,192,128]{3,2,0,1:T(8,128)(2,1)S(1)} %fusion.78), channel_id=1, source_target_pairs={{0,16},{16,32},{32,48},{48,64},{64,80},{80,96},{96,112},{1,17},{17... | collective-permute-start | bytes 1179656 | tf_op jit(solution)/shard_map/ppermute | solution.py:15
  93.7 1.9 collective-permute-start.6
  95.7 3.2 fusion.204
  102.8 2.4 copy.263
  105.2 2.3 copy.259
  107.5 2.3 copy.267
  109.8 2.3 copy.280
  112.2 2.3 copy.276
  117.2 4.3 collective-permute-start.1
  123.7 4.2 collective-permute-start.7
  130.0 2.2 copy.411
  134.8 2.2 copy.410
  139.6 2.2 copy.412
  150.6 30.2 %psum.72 = f32[2,32]{1,0:T(2,128)S(1)} all-reduce(f32[2,32]{1,0:T(2,128)S(1)} %reduce_sum.193), channel_id=1, replica_groups=mesh['tm'=8,'space'=16] {'space'}, use_global_device_ids=true, to_apply=%region_12.13 | all-reduce | flops 64 | bytes 512 | tf_op jit(solution)/shard_map/psum | solution.py:122
  185.5 29.7 %psum.73 = f32[2,32]{1,0:T(2,128)} all-reduce(f32[2,32]{1,0:T(2,128)S(1)} %reduce_sum.196), channel_id=1, replica_groups=mesh['tm'=8,'space'=16] {'space'}, use_global_device_ids=true, to_apply=%region_15.16 | all-reduce | flops 64 | bytes 512 | tf_op jit(solution)/shard_map/psum | solution.py:124
  219.4 2.2 copy.417
  224.2 2.2 copy.416
  229.0 2.2 copy.418
  239.6 2.9 fusion.207
  243.6 2.0 copy.296
  245.9 30.2 %all-reduce.5 = (f32[2,32]{1,0:T(2,128)S(1)}, f32[2,32]{1,0:T(2,128)S(1)}) all-reduce(f32[2,32]{1,0:T(2,128)S(1)} %reduce_sum.205, f32[2,32]{1,0:T(2,128)S(1)} %reduce_sum.202), channel_id=1, replica_groups=mesh['tm'=8,'space'=16] {'space'}, use_global_device_ids=true, to_apply=%region_24.25 | all-reduce | flops 128 | bytes 1024 | tf_op jit(solution)/shard_map/psum | solution.py:139
  309.0 2.1 copy.404
  311.1 26.0 %collective-permute-start.3 = (bf16[2,4,192,128]{3,2,0,1:T(8,128)(2,1)}, bf16[2,4,192,128]{3,2,0,1:T(8,128)(2,1)}, u32[]{:S(2)}, u32[]{:S(2)}) collective-permute-start(bf16[2,4,192,128]{3,2,0,1:T(8,128)(2,1)} %bitcast.410), channel_id=1, source_target_pairs={{0,16},{16,32},{32,48},{48,64},{64,80},{80,96},{96,112},{1,17},{17... | collective-permute-start | bytes 1179656 | tf_op jit(solution)/shard_map/ppermute | solution.py:15
  337.0 1.9 convolution_bitcast_fusion.53
  347.5 5.8 concatenate.60
  356.5 4.2 collective-permute-start.4
  360.7 2.0 convolution_bitcast_fusion.16
  362.7 1.9 convolution_bitcast_fusion.40
  383.3 1.9 convolution_bitcast_fusion.47
  385.2 1.9 convolution_bitcast_fusion.46
  387.2 1.9 convolution_bitcast_fusion.45
  393.1 6.0 concatenate.63
  399.2 1.9 collective-permute-start.9
  401.2 7.6 %collective-permute-done.9 = bf16[2,4,192,128]{3,2,0,1:T(8,128)(2,1)S(1)} collective-permute-done((bf16[2,4,192,128]{3,2,0,1:T(8,128)(2,1)S(1)}, bf16[2,4,192,128]{3,2,0,1:T(8,128)(2,1)S(1)}, u32[]{:S(2)}, u32[]{:S(2)}) %collective-permute-start.9) | collective-permute-done | bytes 393248 | tf_op jit(solution)/shard_map/ppermute | solution.py:15
  410.1 4.7 collective-permute-start.10
  416.1 4.3 collective-permute-done.11
  424.6 2.3 copy.419
  428.6 2.3 copy.421
  444.0 31.7 %all-reduce.4 = (f32[2,32]{1,0:T(2,128)S(1)}, f32[2,32]{1,0:T(2,128)S(1)}) all-reduce(f32[2,32]{1,0:T(2,128)S(1)} %reduce_sum.211, f32[2,32]{1,0:T(2,128)S(1)} %reduce_sum.208), channel_id=1, replica_groups=mesh['tm'=8,'space'=16] {'space'}, use_global_device_ids=true, to_apply=%region_30.31 | all-reduce | flops 128 | bytes 1024 | tf_op jit(solution)/shard_map/psum | solution.py:139
  477.4 2.3 copy.414
  480.5 3.0 copy.413
  483.5 1.9 pad.15.clone
  485.4 3.0 copy.415
  488.5 1.9 pad.19.clone
  499.0 41.3 %all-reduce.11.cloned.1.call-done = (f32[5184,192]{0,1:T(8,128)}, f32[5184,192]{0,1:T(8,128)}) async-done(((f32[5184,192]{0,1:T(8,128)}, f32[5184,192]{0,1:T(8,128)}), (f32[5184,192]{0,1:T(8,128)}, f32[5184,192]{0,1:T(8,128)})) %all-reduce.11.cloned.1.call-update) | async-done | bytes 7962640
  545.9 56.9 %all-reduce.13.cloned.1.call-done = (f32[324,192]{0,1:T(8,128)}, f32[324,192]{0,1:T(8,128)}) async-done(((f32[324,192]{0,1:T(8,128)}, f32[324,192]{0,1:T(8,128)}), (f32[324,192]{0,1:T(8,128)}, f32[324,192]{0,1:T(8,128)})) %all-reduce.13.cloned.1.call-update) | async-done | bytes 497680 | tf_op jit(solution)/shard_map/psum | solution.py:192
  (384 shorter events, 160.6 us)
Async XLA Ops:
  7.2 67.5 %copy-start.8 = (bf16[2,4,192,128]{3,2,1,0:T(8,128)(2,1)S(1)}, bf16[2,4,192,128]{3,2,1,0:T(8,128)(2,1)}, u32[]{:S(2)}) copy-start(bf16[2,4,192,128]{3,2,1,0:T(8,128)(2,1)} %param.9) | copy-start | bytes 1179652
  7.2 86.3 %copy-start = (bf16[2,4,192,128]{3,2,1,0:T(8,128)(2,1)S(1)}, bf16[2,4,192,128]{3,2,1,0:T(8,128)(2,1)}, u32[]{:S(2)}) copy-start(bf16[2,4,192,128]{3,2,1,0:T(8,128)(2,1)} %param.16) | copy-start | bytes 1179652
  7.2 533.1 %all-reduce.11.cloned.1.call-start = ((), (), s32[]{:S(2)}) async-start(), calls=%async_computation | async-start | bytes 16121856
  75.7 52.2 %copy-start.10 = (bf16[2,4,192,128]{3,2,0,1:T(8,128)(2,1)}, bf16[2,4,192,128]{3,2,0,1:T(8,128)(2,1)S(1)}, u32[]{:S(2)}) copy-start(bf16[2,4,192,128]{3,2,0,1:T(8,128)(2,1)S(1)} %fusion.78) | copy-start | bytes 1179652
  75.7 40.1 %collective-permute-start = (bf16[2,4,192,128]{3,2,0,1:T(8,128)(2,1)S(1)}, bf16[2,4,192,128]{3,2,0,1:T(8,128)(2,1)S(1)}, u32[]{:S(2)}, u32[]{:S(2)}) collective-permute-start(bf16[2,4,192,128]{3,2,0,1:T(8,128)(2,1)S(1)} %fusion.78), channel_id=1, source_target_pairs={{0,16},{16,32},{32,48},{48,64},{64,80},{80,96},{96,112},{1,17},{17... | collective-permute-start | bytes 1179656 | tf_op jit(solution)/shard_map/ppermute | solution.py:15
  93.7 27.8 %collective-permute-start.6 = (bf16[2,4,192,128]{3,2,0,1:T(8,128)(2,1)S(1)}, bf16[2,4,192,128]{3,2,0,1:T(8,128)(2,1)S(1)}, u32[]{:S(2)}, u32[]{:S(2)}) collective-permute-start(bf16[2,4,192,128]{3,2,0,1:T(8,128)(2,1)S(1)} %get-tuple-element.75), channel_id=1, source_target_pairs={{16,0},{32,16},{48,32},{64,48},{80,64},{96,80},{112,96},{17,1},{33... | collective-permute-start | bytes 1179656 | tf_op jit(solution)/shard_map/ppermute | solution.py:15
  95.7 3.2 copy-start.23
  102.2 13.6 %copy-start.61 = (bf16[2]{0:T(256)(128)(2,1)}, bf16[2]{0:T(256)(128)(2,1)S(1)}, u32[]{:S(2)}) copy-start(bf16[2]{0:T(256)(128)(2,1)S(1)} %get-tuple-element.79) | copy-start | bytes 16
  115.9 12.1 %copy-start.17 = (bf16[2,4,192,128]{3,2,0,1:T(8,128)(2,1)}, bf16[2,4,192,128]{3,2,0,1:T(8,128)(2,1)S(1)}, u32[]{:S(2)}) copy-start(bf16[2,4,192,128]{3,2,0,1:T(8,128)(2,1)S(1)} %collective-permute-done) | copy-start | bytes 1179652
  115.9 12.0 %collective-permute-start.2 = (bf16[4,1,192,128]{3,2,0,1:T(8,128)(2,1)S(1)}, bf16[4,1,192,128]{3,2,0,1:T(8,128)(2,1)S(1)}, u32[]{:S(2)}, u32[]{:S(2)}) collective-permute-start(bf16[4,1,192,128]{3,2,0,1:T(8,128)(2,1)S(1)} %get-tuple-element.70), channel_id=1, source_target_pairs={{1,0},{2,1},{3,2},{4,3},{5,4},{6,5},{7,6},{8,7},{9,8},{10,9},{11,1... | collective-permute-start | bytes 589832 | tf_op jit(solution)/shard_map/ppermute | solution.py:28
  117.2 10.7 %collective-permute-start.1 = (bf16[4,1,192,128]{3,2,0,1:T(8,128)(2,1)S(1)}, bf16[4,1,192,128]{3,2,0,1:T(8,128)(2,1)S(1)}, u32[]{:S(2)}, u32[]{:S(2)}) collective-permute-start(bf16[4,1,192,128]{3,2,0,1:T(8,128)(2,1)S(1)} %get-tuple-element.69), channel_id=1, source_target_pairs={{0,1},{1,2},{2,3},{3,4},{4,5},{5,6},{6,7},{7,8},{8,9},{9,10},{10,1... | collective-permute-start | bytes 589832 | tf_op jit(solution)/shard_map/ppermute | solution.py:26
  121.6 6.3 %copy-start.19 = (bf16[4,4,192,128]{3,2,0,1:T(8,128)(2,1)}, bf16[4,4,192,128]{3,2,0,1:T(8,128)(2,1)S(1)}, u32[]{:S(2)}) copy-start(bf16[4,4,192,128]{3,2,0,1:T(8,128)(2,1)S(1)} %constant_dynamic-update-slice_fusion) | copy-start | bytes 2359300
  122.4 95.0 %collective-permute-start.8 = (bf16[4,1,192,128]{3,2,0,1:T(8,128)(2,1)}, bf16[4,1,192,128]{3,2,0,1:T(8,128)(2,1)S(1)}, u32[]{:S(2)}, u32[]{:S(2)}) collective-permute-start(bf16[4,1,192,128]{3,2,0,1:T(8,128)(2,1)} %get-tuple-element.66), channel_id=1, source_target_pairs={{1,0},{2,1},{3,2},{4,3},{5,4},{6,5},{7,6},{8,7},{9,8},{10,9},{11,1... | collective-permute-start | bytes 589832 | tf_op jit(solution)/shard_map/ppermute | solution.py:28
  123.7 93.7 %collective-permute-start.7 = (bf16[4,1,192,128]{3,2,0,1:T(8,128)(2,1)}, bf16[4,1,192,128]{3,2,0,1:T(8,128)(2,1)S(1)}, u32[]{:S(2)}, u32[]{:S(2)}) collective-permute-start(bf16[4,1,192,128]{3,2,0,1:T(8,128)(2,1)} %get-tuple-element.65), channel_id=1, source_target_pairs={{0,1},{1,2},{2,3},{3,4},{4,5},{5,6},{6,7},{7,8},{8,9},{9,10},{10,1... | collective-permute-start | bytes 589832 | tf_op jit(solution)/shard_map/ppermute | solution.py:26
  143.9 1.6 copy-start.25
  144.1 1.5 copy-start.32
  144.1 1.6 copy-start.41
  145.7 1.5 copy-start.39
  181.0 1.7 copy-start.4
  181.2 1.8 copy-start.6
  183.0 34.5 %copy-start.20 = (bf16[4,4,192,128]{3,2,0,1:T(8,128)(2,1)S(1)}, bf16[4,4,192,128]{3,2,0,1:T(8,128)(2,1)}, u32[]{:S(2)}) copy-start(bf16[4,4,192,128]{3,2,0,1:T(8,128)(2,1)} %copy-done.19) | copy-start | bytes 2359300
  233.4 1.7 copy-start.7
  233.4 1.7 copy-start.71
  233.4 1.7 copy-start.72
  235.0 1.6 copy-start.5
  235.1 2.9 copy-start.1
  238.0 1.6 copy-start.33
  245.5 31.0 %copy-start.62 = (bf16[2]{0:T(256)(128)(2,1)S(1)}, bf16[2]{0:T(256)(128)(2,1)}, u32[]{:S(2)}) copy-start(bf16[2]{0:T(256)(128)(2,1)} %copy-done.61) | copy-start | bytes 16
  276.7 1.6 copy-start.14
  311.0 27.9 %copy-start.18 = (bf16[2,4,192,128]{3,2,0,1:T(8,128)(2,1)S(1)}, bf16[2,4,192,128]{3,2,0,1:T(8,128)(2,1)}, u32[]{:S(2)}) copy-start(bf16[2,4,192,128]{3,2,0,1:T(8,128)(2,1)} %copy-done.17) | copy-start | bytes 1179652
  311.1 28.9 %copy-start.12 = (bf16[2,4,192,128]{3,2,0,1:T(8,128)(2,1)S(1)}, bf16[2,4,192,128]{3,2,0,1:T(8,128)(2,1)}, u32[]{:S(2)}) copy-start(bf16[2,4,192,128]{3,2,0,1:T(8,128)(2,1)} %copy-done.10) | copy-start | bytes 1179652
  311.1 28.9 %copy-start.58 = (bf16[4,1,192,128]{3,2,0,1:T(8,128)(2,1)S(1)}, bf16[4,1,192,128]{3,2,0,1:T(8,128)(2,1)}, u32[]{:S(2)}) copy-start(bf16[4,1,192,128]{3,2,0,1:T(8,128)(2,1)} %copy-done.57) | copy-start | bytes 589828
  311.1 43.2 %collective-permute-start.3 = (bf16[2,4,192,128]{3,2,0,1:T(8,128)(2,1)}, bf16[2,4,192,128]{3,2,0,1:T(8,128)(2,1)}, u32[]{:S(2)}, u32[]{:S(2)}) collective-permute-start(bf16[2,4,192,128]{3,2,0,1:T(8,128)(2,1)} %bitcast.410), channel_id=1, source_target_pairs={{0,16},{16,32},{32,48},{48,64},{64,80},{80,96},{96,112},{1,17},{17... | collective-permute-start | bytes 1179656 | tf_op jit(solution)/shard_map/ppermute | solution.py:15
  346.0 1.5 copy-start.52
  347.5 5.8 copy-start.13
  355.2 9.3 %collective-permute-start.5 = (bf16[4,1,192,128]{3,2,0,1:T(8,128)(2,1)S(1)}, bf16[4,1,192,128]{3,2,0,1:T(8,128)(2,1)S(1)}, u32[]{:S(2)}, u32[]{:S(2)}) collective-permute-start(bf16[4,1,192,128]{3,2,0,1:T(8,128)(2,1)S(1)} %get-tuple-element.68), channel_id=1, source_target_pairs={{1,0},{2,1},{3,2},{4,3},{5,4},{6,5},{7,6},{8,7},{9,8},{10,9},{11,1... | collective-permute-start | bytes 589832 | tf_op jit(solution)/shard_map/ppermute | solution.py:28
  356.5 8.0 %collective-permute-start.4 = (bf16[4,1,192,128]{3,2,0,1:T(8,128)(2,1)S(1)}, bf16[4,1,192,128]{3,2,0,1:T(8,128)(2,1)S(1)}, u32[]{:S(2)}, u32[]{:S(2)}) collective-permute-start(bf16[4,1,192,128]{3,2,0,1:T(8,128)(2,1)S(1)} %get-tuple-element.67), channel_id=1, source_target_pairs={{0,1},{1,2},{2,3},{3,4},{4,5},{5,6},{6,7},{7,8},{8,9},{9,10},{10,1... | collective-permute-start | bytes 589832 | tf_op jit(solution)/shard_map/ppermute | solution.py:26
  399.2 15.6 %copy-start.74 = (u32[128]{0:T(128)S(1)}, u32[128]{0:T(128)}, u32[]{:S(2)}) copy-start(u32[128]{0:T(128)} %constant.116) | copy-start | bytes 1540
  399.2 203.6 %all-reduce.13.cloned.1.call-start = ((), (), s32[]{:S(2)}) async-start(), calls=%async_computation.1 | async-start | bytes 1179648 | tf_op jit(solution)/shard_map/psum | solution.py:192
  399.2 9.5 %collective-permute-start.9 = (bf16[2,4,192,128]{3,2,0,1:T(8,128)(2,1)S(1)}, bf16[2,4,192,128]{3,2,0,1:T(8,128)(2,1)S(1)}, u32[]{:S(2)}, u32[]{:S(2)}) collective-permute-start(bf16[2,4,192,128]{3,2,0,1:T(8,128)(2,1)S(1)} %bitcast.403), channel_id=1, source_target_pairs={{16,0},{32,16},{48,32},{64,48},{80,64},{96,80},{112,96},{17,1},{33... | collective-permute-start | bytes 1179656 | tf_op jit(solution)/shard_map/ppermute | solution.py:15
  408.8 11.6 %collective-permute-start.11 = (bf16[4,1,192,128]{3,2,0,1:T(8,128)(2,1)S(1)}, bf16[4,1,192,128]{3,2,0,1:T(8,128)(2,1)S(1)}, u32[]{:S(2)}, u32[]{:S(2)}) collective-permute-start(bf16[4,1,192,128]{3,2,0,1:T(8,128)(2,1)S(1)} %get-tuple-element.64), channel_id=1, source_target_pairs={{1,0},{2,1},{3,2},{4,3},{5,4},{6,5},{7,6},{8,7},{9,8},{10,9},{11,1... | collective-permute-start | bytes 589832 | tf_op jit(solution)/shard_map/ppermute | solution.py:28
  410.1 11.7 %collective-permute-start.10 = (bf16[4,1,192,128]{3,2,0,1:T(8,128)(2,1)S(1)}, bf16[4,1,192,128]{3,2,0,1:T(8,128)(2,1)S(1)}, u32[]{:S(2)}, u32[]{:S(2)}) collective-permute-start(bf16[4,1,192,128]{3,2,0,1:T(8,128)(2,1)S(1)} %get-tuple-element.63), channel_id=1, source_target_pairs={{0,1},{1,2},{2,3},{3,4},{4,5},{5,6},{6,7},{7,8},{8,9},{9,10},{10,1... | collective-permute-start | bytes 589832 | tf_op jit(solution)/shard_map/ppermute | solution.py:26
  416.1 5.8 copy-start.66
  416.1 5.8 copy-start.68
  434.9 1.5 copy-start.42
  436.4 1.6 copy-start.40
  491.3 1.9 copy-start.38
  493.6 1.5 copy-start.36
  (44 other events, 51.5 us)
Sparse Core Ops, SparseCore 0:
  399.3 140.9 all-reduce.10
  544.1 58.6 all-reduce.12
where the time goes:
time: 622 us; the launch traced here: 613 us
  blocking collectives  186 us (30%)
  local copies, waits for them, and re-layouts  113 us (18%)
  waiting for transfers between devices  111 us (18%)
  matrix products  78.7 us (13%)
  starting transfers between devices  70.2 us (11%)
  other arithmetic  37.6 us (6%)
  between operations  16.6 us (3%)
    psum x2, blocking collectives, norm_forward(): lax.psum(jnp.sum(grouped, axis=(1, 3, 4)), 'space') / cell_count  65.9 us
    psum x2, blocking collectives, norm_adjoint(): lax.psum((jnp.sum(grad_norm, axis=(1, 3, 4)), jnp.sum(grad_norm * norm_gr...  61.8 us
    dot_general x54, matrix products, weight_gradient(): jnp.einsum('thcw,thow->co', window_piece, masked, preferred_element_type=...  60.5 us
    psum x2, blocking collectives, norm_forward(): lax.psum(jnp.sum(centered * centered, axis=(1, 3, 4)), 'space') / cell_count  58.2 us
    psum x1, waiting for transfers between devices, shards(): summed_one, summed_two = lax.psum((local_grad_one, local_grad_two), 'tm')  56.9 us
    unnamed x180, local copies, waits for them, and re-layouts  50.7 us
    ppermute x4, starting transfers between devices, from_behind(): return lax.ppermute(block, axis, route)  47.6 us
    unnamed x3, waiting for transfers between devices  41.3 us
  transfers between devices with their start and end apart: 14, of which 5 were waited for; matrix products, arithmetic and copies ran while one was open for 18% of the time, Pallas kernels for 0%

commit v1 on v0

v1 whole, which is shorter than its diff:
```python
import functools

import jax
import jax.numpy as jnp
from jax import lax
from jax.experimental import pallas as pl
from jax.experimental.pallas import tpu as pltpu
from jax.sharding import PartitionSpec as P

GROUPS = 32
NORM_EPSILON = 1e-05

C = 192
W = 128
PER_GROUP = C // GROUPS
ROWS = 4
OWN = 2
TAP_ROWS = 3 * C
DEPTH = 3 * TAP_ROWS
ALL_TAPS = 3 * DEPTH
SPACE = 16
TM = 8
SHARE = ALL_TAPS // SPACE
PACKED = 512
LOCAL_COUNT = ROWS * PER_GROUP * W
FULL_COUNT = LOCAL_COUNT * SPACE

F32 = jnp.float32
BF16 = jnp.bfloat16
EXACT = lax.Precision.HIGHEST


def call(kernel, out_shape, operands, smem=0, scratch=(), flops=0, **extra):
    nbytes = sum(x.size * x.dtype.itemsize for x in operands)
    return pl.pallas_call(
        kernel,
        out_shape=out_shape,
        in_specs=[pl.BlockSpec(memory_space=pltpu.SMEM)] * smem
        + [pl.BlockSpec(memory_space=pltpu.VMEM)] * (len(operands) - smem),
        out_specs=jax.tree.map(lambda _: pl.BlockSpec(memory_space=pltpu.VMEM), out_shape),
        scratch_shapes=list(scratch),
        compiler_params=pltpu.CompilerParams(vmem_limit_bytes=48 * 1024 * 1024),
        cost_estimate=pl.CostEstimate(flops=flops, bytes_accessed=nbytes, transcendentals=0),
        **extra,
    )(*operands)


def lane_ids(rows=C):
    return lax.broadcasted_iota(jnp.int32, (rows, W), 1)


def membership():
    channel = lax.broadcasted_iota(jnp.int32, (C, W), 0)
    group = lane_ids()
    inside = (channel >= group * PER_GROUP) & (channel < (group + 1) * PER_GROUP)
    return inside.astype(F32)


def to_groups(columns):
    lanes = lane_ids()
    packed = jnp.zeros((C, W), F32)
    for i, column in enumerate(columns):
        packed = jnp.where(lanes == i, column, packed)
    summed = lax.dot_general(
        packed, membership(), (((0,), (0,)), ((), ())), precision=EXACT, preferred_element_type=F32
    )
    return summed[:8]


def to_channels(table):
    return lax.dot_general(
        membership(), table, (((1,), (1,)), ((), ())), precision=EXACT, preferred_element_type=F32
    )


def merged_stats(parts_ref, frames):
    means = parts_ref[:, 0:4, :]
    mean = jnp.sum(means, axis=0) * (1.0 / SPACE)
    spread = jnp.sum((means - mean[None]) ** 2, axis=0) * float(LOCAL_COUNT)
    variance = (jnp.sum(parts_ref[:, 4:8, :], axis=0) + spread) * (1.0 / FULL_COUNT)
    inverse = lax.rsqrt(variance + NORM_EPSILON)
    return to_channels(jnp.concatenate([mean, inverse], axis=0))


def local_stats(blocks):
    sums = []
    for rows in blocks:
        total = rows[0]()
        for row in rows[1:]:
            total = total + row()
        sums.append(jnp.sum(total, axis=1, keepdims=True))
    means = to_groups(sums) * (1.0 / LOCAL_COUNT)
    spread = to_channels(means)
    squares = []
    for f, rows in enumerate(blocks):
        total = None
        for row in rows:
            centered = row() - spread[:, f : f + 1]
            total = centered * centered if total is None else total + centered * centered
        squares.append(jnp.sum(total, axis=1, keepdims=True))
    deviations = to_groups(squares)
    return jnp.concatenate([means[:4], deviations[:4]], axis=0)


def store_shifted(cols_ref, h, f, field):
    lanes = lane_ids()
    before = jnp.where(lanes == 0, 0.0, pltpu.roll(field, 1, 1))
    after = jnp.where(lanes == W - 1, 0.0, pltpu.roll(field, W - 1, 1))
    for s, part in enumerate((before, field, after)):
        start = h * TAP_ROWS + s * C
        cols_ref[start : start + C, f * W : (f + 1) * W] = part.astype(BF16)


def conv_rows(kernels, cols_ref, factors, finish):
    wide = lax.broadcasted_iota(jnp.int32, (C, 2 * W), 1) < W
    for h in range(ROWS):
        total = None
        for k in range(3):
            part = jnp.dot(
                kernels[k],
                cols_ref[h * TAP_ROWS : h * TAP_ROWS + DEPTH, k * W : (k + 2) * W],
                preferred_element_type=F32,
            )
            if factors[k] is not None:
                part = part * jnp.where(wide, factors[k][0], factors[k][1])
            total = part if total is None else total + part
        finish(h, total)


def loader(own_ref, beside_ref, top_ref, bottom_ref, own_first, beside_row0):
    def load(f, h):
        if h == 0:
            return top_ref[beside_row0 + f].astype(F32)
        if h == ROWS + 1:
            return bottom_ref[beside_row0 + f].astype(F32)
        if own_first:
            block = own_ref[f, h - 1] if f < OWN else beside_ref[f - OWN, h - 1]
        else:
            block = beside_ref[f, h - 1] if f < OWN else own_ref[f - OWN, h - 1]
        return block.astype(F32)

    return load


def stats_kernel(own_ref, prev_ref, out_ref):
    def row(ref, f, h):
        return lambda: ref[f, h].astype(F32)

    blocks = [[row(prev_ref, f, h) for h in range(ROWS)] for f in range(OWN)]
    blocks += [[row(own_ref, f, h) for h in range(ROWS)] for f in range(OWN)]
    out_ref[...] = jnp.broadcast_to(local_stats(blocks)[None], (SPACE, 8, W))


def silu_of(pre):
    return pre / (1.0 + jnp.exp(-pre))


def conv_one_kernel(
    table_ref, parts_ref, own_ref, prev_ref, top_ref, bottom_ref, param_ref, weight_ref,
    cols_ref, conv_ref, out_ref,
):
    stats = merged_stats(parts_ref, 4)
    gain, bias = param_ref[:, 0:1], param_ref[:, 1:2]
    load = loader(own_ref, prev_ref, top_ref, bottom_ref, False, 0)
    for f in range(4):
        mean = jnp.broadcast_to(stats[:, f : f + 1], (C, W))
        scale = jnp.broadcast_to(stats[:, 4 + f : 5 + f] * gain, (C, W))
        shift = jnp.broadcast_to(bias, (C, W))
        for h in range(ROWS + 2):
            active = silu_of((load(f, h) - mean) * scale + shift)
            if h == 0:
                active = active * table_ref[12]
            if h == ROWS + 1:
                active = active * table_ref[13]
            store_shifted(cols_ref, h, f, active)
    kernels = [weight_ref[:, k * DEPTH : (k + 1) * DEPTH] for k in range(3)]
    factors = [(table_ref[(2 - k) * 4], table_ref[(2 - k) * 4 + 1]) for k in range(2)] + [None]

    def finish(h, total):
        conv_ref[0, h] = total[:, :W]
        conv_ref[1, h] = total[:, W:]

    conv_rows(kernels, cols_ref, factors, finish)

    def row(f, h):
        return lambda: conv_ref[f, h]

    blocks = [[row(f, h) for h in range(ROWS)] for f in range(OWN)]
    out_ref[...] = jnp.broadcast_to(local_stats(blocks)[None], (SPACE, 8, W))


def turn_kernel(one_ref, two_ref, out_one_ref, out_two_ref):
    for src, dst in ((one_ref, out_one_ref), (two_ref, out_two_ref)):
        for tap in range(27):
            k, spot = divmod(26 - tap, 9)
            block = src[:, tap * C : (tap + 1) * C]
            dst[k, :, spot * C : (spot + 1) * C] = block.T


def adjoint_kernel(table_ref, own_ref, next_ref, top_ref, bottom_ref, weight_ref, out_ref, cols_ref, *, first):
    load = loader(own_ref, next_ref, top_ref, bottom_ref, True, first)
    for f in range(4):
        for h in range(ROWS + 2):
            store_shifted(cols_ref, h, f, load(f, h))
    factors = [None] + [(table_ref[j * 4 + j], table_ref[j * 4 + j + 1]) for j in (1, 2)]

    def finish(h, total):
        out_ref[0, h] = total[:, :W]
        out_ref[1, h] = total[:, W:]

    conv_rows([weight_ref[j] for j in range(3)], cols_ref, factors, finish)


def norm_grad_rows(f, h, value, upstream, mean, inverse, gain, bias):
    normalized = (value - mean) * inverse
    pre = normalized * gain + bias
    sigmoid = 1.0 / (1.0 + jnp.exp(-pre))
    grad = upstream * (sigmoid * (1.0 + pre * (1.0 - sigmoid))) * gain
    return normalized, grad, pre * sigmoid


def norm_grad(load, upstream_ref, stats, first, gain, bias, grad_ref, norm_ref, active_ref):
    plain, weighted = [], []
    for f in range(OWN):
        mean = jnp.broadcast_to(stats[:, first + f : first + f + 1], (C, W))
        inverse = jnp.broadcast_to(stats[:, 4 + first + f : 5 + first + f], (C, W))
        gain_wide = jnp.broadcast_to(gain, (C, W))
        bias_wide = jnp.broadcast_to(bias, (C, W))
        sums = None
        for h in range(ROWS):
            normalized, grad, active = norm_grad_rows(
                f, h, load(f, h), upstream_ref[f, h], mean, inverse, gain_wide, bias_wide
            )
            grad_ref[f, h] = grad
            norm_ref[f, h] = normalized
            if active_ref is not None:
                active_ref[f, h] = active.astype(BF16)
            pair = (grad, grad * normalized)
            sums = pair if sums is None else (sums[0] + pair[0], sums[1] + pair[1])
        plain.append(jnp.sum(sums[0], axis=1, keepdims=True))
        weighted.append(jnp.sum(sums[1], axis=1, keepdims=True))
    return to_groups(plain + weighted)


def norm_two_kernel(parts_ref, conv_ref, upstream_ref, param_ref, active_ref, grad_ref, norm_ref, out_ref):
    stats = merged_stats(parts_ref, 2)
    sums = norm_grad(
        lambda f, h: conv_ref[f, h], upstream_ref, stats, 0, param_ref[:, 2:3], param_ref[:, 3:4],
        grad_ref, norm_ref, active_ref,
    )
    out_ref[...] = jnp.broadcast_to(sums[None], (SPACE, 8, W))


def norm_one_kernel(parts_ref, own_ref, upstream_ref, param_ref, grad_ref, norm_ref, out_ref):
    stats = merged_stats(parts_ref, 4)
    sums = norm_grad(
        lambda f, h: own_ref[f, h].astype(F32), upstream_ref, stats, 2, param_ref[:, 0:1], param_ref[:, 1:2],
        grad_ref, norm_ref, None,
    )
    out_ref[...] = jnp.broadcast_to(sums[None], (SPACE, 8, W))


def field_grad(parts_ref, sums_ref, grad_ref, norm_ref, first, finish):
    stats = merged_stats(parts_ref, 4)
    totals = to_channels(jnp.sum(sums_ref[...], axis=0) * (1.0 / FULL_COUNT))
    for f in range(OWN):
        inverse = jnp.broadcast_to(stats[:, 4 + first + f : 5 + first + f], (C, W))
        plain = jnp.broadcast_to(totals[:, f : f + 1], (C, W))
        weighted = jnp.broadcast_to(totals[:, OWN + f : OWN + f + 1], (C, W))
        for h in range(ROWS):
            finish(f, h, inverse * (grad_ref[f, h] - plain - norm_ref[f, h] * weighted))


def grad_conv_kernel(parts_ref, sums_ref, grad_ref, norm_ref, out_ref):
    def finish(f, h, value):
        out_ref[f, h] = value.astype(BF16)

    field_grad(parts_ref, sums_ref, grad_ref, norm_ref, 0, finish)


def input_grad_kernel(parts_ref, sums_ref, grad_ref, norm_ref, cot_ref, out_ref):
    def finish(f, h, value):
        out_ref[f, h] = (cot_ref[f, h].astype(F32) + value).astype(BF16)

    field_grad(parts_ref, sums_ref, grad_ref, norm_ref, 2, finish)


def weight_grad(table_ref, cols_ref, grad_ref, dense_ref, out_ref):
    wide = lax.broadcasted_iota(jnp.int32, (C, 2 * W), 1) < W
    rows = [jnp.concatenate([grad_ref[0, h], grad_ref[1, h]], axis=1) for h in range(ROWS)]
    for k in range(3):
        if k < 2:
            factor = jnp.where(wide, table_ref[(2 - k) * 4], table_ref[(2 - k) * 4 + 1])
            masked = [(row.astype(F32) * factor).astype(BF16) for row in rows]
        else:
            masked = rows
        total = None
        for h in range(ROWS):
            part = lax.dot_general(
                cols_ref[h * TAP_ROWS : h * TAP_ROWS + DEPTH, k * W : (k + 2) * W],
                masked[h],
                (((1,), (1,)), ((), ())),
                preferred_element_type=F32,
            )
            if h == 0:
                dense_ref[k * DEPTH : (k + 1) * DEPTH, :] = part
            else:
                dense_ref[k * DEPTH : (k + 1) * DEPTH, :] += part
    half = SHARE // 2
    rest = C - W
    for s in range(SPACE):
        low = dense_ref[s * SHARE : (s + 1) * SHARE, 0:W]
        high = jnp.concatenate(
            [
                dense_ref[s * SHARE : s * SHARE + half, W:C],
                dense_ref[s * SHARE + half : (s + 1) * SHARE, W:C],
            ],
            axis=1,
        )
        spare = jnp.zeros((PACKED - SHARE - half, W), F32)
        packed = jnp.concatenate([low, high, spare], axis=0).astype(out_ref.dtype)
        piece = PACKED // TM
        for i in range(TM):
            out_ref[i, s] = packed[i * piece : (i + 1) * piece]


def weight_one_kernel(table_ref, cols_ref, grad_ref, out_ref, dense_ref):
    weight_grad(table_ref, cols_ref, grad_ref, dense_ref, out_ref)


def conv_two_kernel(
    table_ref, own_ref, prev_ref, top_ref, bottom_ref, weight_ref, input_ref, cot_ref,
    decoded_ref, out_ref, cols_ref, dense_ref,
):
    load = loader(own_ref, prev_ref, top_ref, bottom_ref, False, 0)
    for f in range(4):
        for h in range(ROWS + 2):
            store_shifted(cols_ref, h, f, load(f, h))
    kernels = [weight_ref[:, k * DEPTH : (k + 1) * DEPTH] for k in range(3)]
    factors = [(table_ref[(2 - k) * 4], table_ref[(2 - k) * 4 + 1]) for k in range(2)] + [None]

    def finish(h, total):
        for f in range(OWN):
            field = input_ref[f, h].astype(F32) + total[:, f * W : (f + 1) * W]
            decoded_ref[f, h] = field.astype(BF16)

    conv_rows(kernels, cols_ref, factors, finish)
    weight_grad(table_ref, cols_ref, cot_ref, dense_ref, out_ref)


def unpack_kernel(one_ref, two_ref, out_one_ref, out_two_ref, *, scale):
    half = SHARE // 2
    for src, dst in ((one_ref, out_one_ref), (two_ref, out_two_ref)):
        dst[:, 0:W] = src[0:SHARE].astype(F32) * scale
        high = src[SHARE : SHARE + half].astype(F32) * scale
        dst[0:half, W:C] = high[:, : C - W]
        dst[half:SHARE, W:C] = high[:, C - W :]


def keep_table(first_frame, frame_count, clip_ends):
    frame_ids = first_frame + jnp.arange(frame_count, dtype=jnp.int32)
    own_clip = jnp.sum((frame_ids[:, None] >= clip_ends[None, :]).astype(jnp.int32), axis=1)
    lagged = [jnp.ones((frame_count,), F32)]
    for lag_size in (1, 2):
        shifted_ids = frame_ids - lag_size
        before_clip = jnp.sum((shifted_ids[:, None] >= clip_ends[None, :]).astype(jnp.int32), axis=1)
        allowed = (shifted_ids >= 0) & (before_clip == own_clip)
        lagged.append(allowed.astype(F32))
    return jnp.stack(lagged)


FORWARD = [(i, i + 1) for i in range(TM - 1)]
BACKWARD = [(i + 1, i) for i in range(TM - 1)]
DOWN = [(i, i + 1) for i in range(SPACE - 1)]
UP = [(i + 1, i) for i in range(SPACE - 1)]


def row_halos(first, second):
    low = jnp.concatenate([first[:, ROWS - 1], second[:, ROWS - 1]], axis=0)
    high = jnp.concatenate([first[:, 0], second[:, 0]], axis=0)
    return lax.ppermute(low, "space", DOWN), lax.ppermute(high, "space", UP)


def swap(parts):
    return lax.all_to_all(parts, "space", 0, 0)


def shape(dims, dtype=F32):
    return jax.ShapeDtypeStruct(dims, dtype)


CONV_FLOPS = 2 * OWN * ROWS * W * ALL_TAPS * C
FIELD = (OWN, ROWS, C, W)
COLS = (6 * TAP_ROWS, 4 * W)


def shards(
    activations,
    weight_one,
    weight_two,
    gain_one,
    bias_one,
    gain_two,
    bias_two,
    cotangent,
    clip_lengths,
):
    clip_ends = jnp.cumsum(clip_lengths)
    row = lax.axis_index("space")
    keeps = keep_table(lax.axis_index("tm") * OWN, 4, clip_ends)
    edges = jnp.stack([row > 0, row < SPACE - 1]).astype(F32)
    table = jnp.concatenate([keeps.reshape(-1), edges])
    params = jnp.stack([gain_one, bias_one, gain_two, bias_two], axis=1)
    turned_one, turned_two = weight_one.T, weight_two.T

    previous = lax.ppermute(activations, "tm", FORWARD)
    following = lax.ppermute(cotangent, "tm", BACKWARD)
    adjoint_one, adjoint_two = call(
        turn_kernel, (shape((3, C, DEPTH), BF16),) * 2, (turned_one, turned_two)
    )
    parts = call(stats_kernel, shape((SPACE, 8, W)), (activations, previous))
    above, below = row_halos(
        jnp.concatenate([previous, activations], axis=0), jnp.concatenate([cotangent, following], axis=0)
    )
    stats_one = swap(parts)
    columns_one, conv_one, parts = call(
        conv_one_kernel,
        (shape(COLS, BF16), shape(FIELD), shape((SPACE, 8, W))),
        (table, stats_one, activations, previous, above, below, params, turned_one),
        smem=1,
        flops=CONV_FLOPS,
    )
    grad_active_two = call(
        functools.partial(adjoint_kernel, first=4),
        shape(FIELD),
        (table, cotangent, following, above, below, adjoint_two),
        smem=1,
        scratch=[pltpu.VMEM(COLS, BF16)],
        flops=CONV_FLOPS,
    )
    stats_two = swap(parts)
    active_two, grad_norm, normalized, parts = call(
        norm_two_kernel,
        (shape(FIELD, BF16), shape(FIELD), shape(FIELD), shape((SPACE, 8, W))),
        (stats_two, conv_one, grad_active_two, params),
    )
    previous_two = lax.ppermute(active_two, "tm", FORWARD)
    sums_two = swap(parts)
    grad_conv_one = call(
        grad_conv_kernel, shape(FIELD, BF16), (stats_two, sums_two, grad_norm, normalized)
    )
    following_one = lax.ppermute(grad_conv_one, "tm", BACKWARD)
    above_two, below_two = row_halos(previous_two, active_two)
    packed = shape((TM, SPACE, PACKED // TM, W))
    local_one = call(
        weight_one_kernel,
        packed,
        (table, columns_one, grad_conv_one),
        smem=1,
        scratch=[pltpu.VMEM((ALL_TAPS, C), F32)],
        flops=CONV_FLOPS,
    )
    above_one, below_one = row_halos(grad_conv_one, following_one)
    decoded, local_two = call(
        conv_two_kernel,
        (shape(FIELD, BF16), packed),
        (table, active_two, previous_two, above_two, below_two, turned_two, activations, cotangent),
        smem=1,
        scratch=[pltpu.VMEM(COLS, BF16), pltpu.VMEM((ALL_TAPS, C), F32)],
        flops=2 * CONV_FLOPS,
    )
    rows = SPACE * PACKED // TM
    shares = [
        lax.psum_scatter(local.reshape(TM * rows, W), "tm", scatter_dimension=0, tiled=True)
        for local in (local_one, local_two)
    ]
    grad_active_one = call(
        functools.partial(adjoint_kernel, first=0),
        shape(FIELD),
        (table, grad_conv_one, following_one, above_one, below_one, adjoint_one),
        smem=1,
        scratch=[pltpu.VMEM(COLS, BF16)],
        flops=CONV_FLOPS,
    )
    grad_norm, normalized, parts = call(
        norm_one_kernel,
        (shape(FIELD), shape(FIELD), shape((SPACE, 8, W))),
        (stats_one, activations, grad_active_one, params),
    )
    sums_one = swap(parts)
    input_grad = call(
        input_grad_kernel, shape(FIELD, BF16), (stats_one, sums_one, grad_norm, normalized, cotangent)
    )
    both = jnp.concatenate([s.reshape(SPACE, PACKED // TM, W) for s in shares], axis=1).astype(BF16)
    summed = jnp.sum(swap(both).astype(F32), axis=0)
    spread = jnp.broadcast_to(summed[None], (TM,) + summed.shape)
    gathered = lax.all_to_all(spread, "tm", 0, 0).reshape(TM, 2, PACKED // TM, W)
    total_cells = OWN * TM * ROWS * SPACE * W
    share_one, share_two = call(
        functools.partial(unpack_kernel, scale=float(total_cells) ** -0.5),
        (shape((SHARE, C)),) * 2,
        (gathered[:, 0].reshape(PACKED, W), gathered[:, 1].reshape(PACKED, W)),
    )
    return (decoded, input_grad, share_one, share_two)


def solution(mesh):
    placed = (
        P("tm", "space", None, None),
        P(),
        P(),
        P(),
        P(),
        P(),
        P(),
        P("tm", "space", None, None),
        P(),
    )
    return jax.shard_map(
        shards,
        mesh=mesh,
        in_specs=placed,
        out_specs=(
            P("tm", "space", None, None),
            P("tm", "space", None, None),
            P("space", None),
            P("space", None),
        ),
        check_vma=False,
    )
```

time: 622 us -> 240 us (0.39); the launches traced: 613 us -> 238 us
  blocking collectives: 186 us -> 12.9 us
  local copies, waits for them, and re-layouts: 113 us -> 17.9 us
  matrix products: 78.7 us -> 0 us
  Pallas kernels: 0 us -> 43.6 us
  other arithmetic: 37.6 us -> 7.07 us
  waiting for transfers between devices: 111 us -> 85.2 us
  starting transfers between devices: 70.2 us -> 57.1 us
    psum x6 -> x0, blocking collectives: 186 us -> none  [the longest x2 65.9 us: norm_forward(): lax.psum(jnp.sum(grouped, axis=(1, 3, 4)), 'space') / cell_count]
    dot_general x54 -> x0, matrix products: 60.5 us -> none  [weight_gradient(): jnp.einsum('thcw,thow->co', window_piece, masked, preferred_element_type=...]
    psum x1 -> x0, waiting for transfers between devices: 56.9 us -> none  [shards(): summed_one, summed_two = lax.psum((local_grad_one, local_grad_two), 'tm')]
    ppermute x12 -> x10, starting transfers between devices: 70.1 us -> 25.5 us  [the longest x6 11.4 us: row_halos(): return (lax.ppermute(low, 'space', DOWN), lax.ppermute(high, 'space', UP))]
    pallas_call x0 -> x12, Pallas kernels: none -> 43.6 us  [call(): pl.pallas_call(kernel, out_shape=out_shape, in_specs=[pl.BlockSpec(memory...]
    unnamed x3 -> x2, waiting for transfers between devices: 41.3 us -> 0.03 us
    unnamed x180 -> x47, local copies, waits for them, and re-layouts: 50.7 us -> 13.6 us
    all_to_all x0 -> x5, starting transfers between devices: none -> 31.3 us  [the longest x4 23.3 us: swap(): return lax.all_to_all(parts, 'space', 0, 0)]
  transfers between devices with their start and end apart: 14 -> 17, of which waited for: 5 -> 10; matrix products, arithmetic and copies ran while one was open for 18% -> 5% of each run, Pallas kernels for 0% -> 11%
where the time goes in v1:
time: 240 us; the launch traced here: 238 us
  waiting for transfers between devices  85.2 us (36%)
  starting transfers between devices  57.1 us (24%)
  Pallas kernels  43.6 us (18%)
  local copies, waits for them, and re-layouts  17.9 us (7%)
  between operations  14.6 us (6%)
  blocking collectives  12.9 us (5%)
  other arithmetic  7.07 us (3%)
    pallas_call x12, Pallas kernels, call(): pl.pallas_call(kernel, out_shape=out_shape, in_specs=[pl.BlockSpec(memory...  43.6 us
    reduce_scatter x2, waiting for transfers between devices, shards(): lax.psum_scatter(local.reshape(TM * rows, W), 'tm', scatter_dimension=0,...  28 us
    all_to_all x4, starting transfers between devices, swap(): return lax.all_to_all(parts, 'space', 0, 0)  23.3 us
    ppermute x6, waiting for transfers between devices, row_halos(): return (lax.ppermute(low, 'space', DOWN), lax.ppermute(high, 'space', UP))  16.1 us
    unnamed x47, local copies, waits for them, and re-layouts  13.6 us
    all_to_all x1, blocking collectives, swap(): return lax.all_to_all(parts, 'space', 0, 0)  12.9 us
    ppermute x6, starting transfers between devices, row_halos(): return (lax.ppermute(low, 'space', DOWN), lax.ppermute(high, 'space', UP))  11.4 us
    all_to_all x4, waiting for transfers between devices, swap(): return lax.all_to_all(parts, 'space', 0, 0)  11.1 us
  transfers between devices with their start and end apart: 17, of which 10 were waited for; matrix products, arithmetic and copies ran while one was open for 5% of the time, Pallas kernels for 11%

profile of v1, /device:TPU:1, one launch (start us, length us, event | category | flops | bytes accessed | tf_op | source)
XLA Modules:
  0.0 238.3 jit_solution(14292688519855087837)
XLA Ops:
  7.2 1.1 copy.71
  8.3 4.5 %collective-permute-start = (bf16[2,4,192,128]{3,2,0,1:T(8,128)(2,1)S(1)}, bf16[2,4,192,128]{3,2,0,1:T(8,128)(2,1)S(1)}, u32[]{:S(2)}, u32[]{:S(2)}) collective-permute-start(bf16[2,4,192,128]{3,2,0,1:T(8,128)(2,1)S(1)} %copy.71), channel_id=1, source_target_pairs={{0,16},{16,32},{32,48},{48,64},{64,80},{80,96},{96,112},{1,17},{17... | collective-permute-start | bytes 1179656 | tf_op jit(solution)/shard_map/ppermute | solution.py:416
  12.8 2.0 fusion.3
  14.8 1.9 collective-permute-start.1
  18.0 6.1 %collective-permute-done.1 = bf16[2,4,192,128]{3,2,0,1:T(8,128)(2,1)S(1)} collective-permute-done((bf16[2,4,192,128]{3,2,0,1:T(8,128)(2,1)}, bf16[2,4,192,128]{3,2,0,1:T(8,128)(2,1)S(1)}, u32[]{:S(2)}, u32[]{:S(2)}) %collective-permute-start.1) | collective-permute-done | bytes 393248 | tf_op jit(solution)/shard_map/ppermute | solution.py:417
  25.0 4.3 %collective-permute-start.2 = (bf16[8,192,128]{2,1,0:T(8,128)(2,1)}, bf16[8,192,128]{2,1,0:T(8,128)(2,1)}, u32[]{:S(2)}, u32[]{:S(2)}) collective-permute-start(bf16[8,192,128]{2,1,0:T(8,128)(2,1)} %pad_maximum_fusion.1), channel_id=1, source_target_pairs={{0,1},{1,2},{2,3},{3,4},{4,5},{5,6},{6,7},{7,8},{8,9},{9,10},{10,1... | collective-permute-start | bytes 1179656 | tf_op jit(solution)/shard_map/ppermute | solution.py:381
  30.1 1.3 collective-permute-start.3
  31.7 1.6 copy-done.3
  33.3 6.0 %shard_map.122 = (bf16[3,192,1728]{2,1,0:T(8,128)(2,1)S(1)}, bf16[3,192,1728]{2,1,0:T(8,128)(2,1)}) custom-call(bf16[192,5184]{1,0:T(8,128)(2,1)S(1)} %bitcast.50, bf16[192,5184]{1,0:T(8,128)(2,1)S(1)} %bitcast.52), custom_call_target="tpu_custom_call" | custom-call | bytes 3981312 | tf_op jit(solution)/shard_map/pallas_call | solution.py:35
  39.3 1.4 copy-done.11
  40.7 2.1 shard_map.120
  42.8 8.0 %all-to-all-start = ((f32[16,8,128]{2,1,0:T(8,128)}), f32[16,8,128]{2,1,0:T(8,128)S(1)}, u32[]{:S(2)}, u32[]{:S(2)}) async-start(f32[16,8,128]{2,1,0:T(8,128)} %shard_map.120), calls=%async_computation | async-start | bytes 131072 | tf_op jit(solution)/shard_map/all_to_all | solution.py:385
  51.7 5.7 %all-to-all-done.parts_ref = f32[16,8,128]{2,1,0:T(8,128)S(1)} async-done(((f32[16,8,128]{2,1,0:T(8,128)}), f32[16,8,128]{2,1,0:T(8,128)S(1)}, u32[]{:S(2)}, u32[]{:S(2)}) %all-to-all-start) | async-done | bytes 65568 | tf_op jit(solution)/shard_map/all_to_all | solution.py:385
  57.4 7.6 %shard_map.121 = (bf16[3456,512]{1,0:T(8,128)(2,1)}, f32[2,4,192,128]{3,2,1,0:T(8,128)S(1)}, f32[16,8,128]{2,1,0:T(8,128)}) custom-call(f32[14]{0:T(128)S(1)} %pad_maximum_fusion.9.table_ref, f32[16,8,128]{2,1,0:T(8,128)S(1)} %all-to-all-done.parts_ref, bf16[2,4,192,128]{3,2,1,0:T(8,128)(2,1)S(1)} %copy-done, bf16[2,4,192,128]{3,2,1,0:T(8,128)(2,1)S(1)} %copy.72.prev_ref, ...), custom_call_target="tpu_custom_call" | custom-call | flops 2038431744 | bytes 3632184 | tf_op jit(solution)/shard_map/pallas_call | solution.py:35
  65.8 3.5 %all-to-all-start.1 = ((f32[16,8,128]{2,1,0:T(8,128)}), f32[16,8,128]{2,1,0:T(8,128)S(1)}, u32[]{:S(2)}, u32[]{:S(2)}) async-start(f32[16,8,128]{2,1,0:T(8,128)} %get-tuple-element.20), calls=%async_computation.1 | async-start | bytes 131072 | tf_op jit(solution)/shard_map/all_to_all | solution.py:385
  69.6 1.0 copy-done.10
  70.6 1.6 copy-done.13
  72.2 3.7 %shard_map.123.upstream_ref = f32[2,4,192,128]{3,2,1,0:T(8,128)S(1)} custom-call(f32[14]{0:T(128)S(1)} %pad_maximum_fusion.9.table_ref, bf16[2,4,192,128]{3,2,1,0:T(8,128)(2,1)S(1)} %copy-done.5, bf16[2,4,192,128]{3,2,1,0:T(8,128)(2,1)S(1)} %copy-done.10, bf16[8,192,128]{2,1,0:T(8,128)(2,1)} %collective-permute-done.2.top_ref, ...), custom_call_target="tpu_custom_call" | custom-call | flops 2038431744 | bytes 3563576 | tf_op jit(solution)/shard_map/pallas_call | solution.py:35
  75.9 1.3 shard_map.124
  78.0 12.9 %all_to_all.30.sums_ref = f32[16,8,128]{2,1,0:T(8,128)S(1)} all-to-all(f32[16,8,128]{2,1,0:T(8,128)S(1)} %get-tuple-element.25), channel_id=1, replica_groups=mesh['tm'=8,'space'=16] {'space'}, dimensions={0} | all-to-all | bytes 131072 | tf_op jit(solution)/shard_map/all_to_all | solution.py:385
  91.5 6.7 %shard_map.130 = f32[8,16,64,128]{3,2,1,0:T(8,128)} custom-call(f32[14]{0:T(128)S(1)} %pad_maximum_fusion.9.table_ref, bf16[3456,512]{1,0:T(8,128)(2,1)S(1)} %copy-done.1, bf16[2,4,192,128]{3,2,1,0:T(8,128)(2,1)S(1)} %shard_map.126.own_ref.grad_ref), custom_call_target="tpu_custom_call" | custom-call | flops 2038431744 | bytes 3932216 | tf_op jit(solution)/shard_map/pallas_call | solution.py:35
  98.3 1.2 copy.80
  99.4 5.7 %collective-permute-start.4 = (bf16[2,4,192,128]{3,2,0,1:T(8,128)(2,1)S(1)}, bf16[2,4,192,128]{3,2,0,1:T(8,128)(2,1)S(1)}, u32[]{:S(2)}, u32[]{:S(2)}) collective-permute-start(bf16[2,4,192,128]{3,2,0,1:T(8,128)(2,1)S(1)} %copy.80), channel_id=1, source_target_pairs={{0,16},{16,32},{32,48},{48,64},{64,80},{80,96},{96,112},{1,17},{17... | collective-permute-start | bytes 1179656 | tf_op jit(solution)/shard_map/ppermute | solution.py:447
  105.2 1.0 slice_bitcast_fusion.8
  106.1 7.1 %collective-permute-done.4 = bf16[2,4,192,128]{3,2,0,1:T(8,128)(2,1)S(1)} collective-permute-done((bf16[2,4,192,128]{3,2,0,1:T(8,128)(2,1)S(1)}, bf16[2,4,192,128]{3,2,0,1:T(8,128)(2,1)S(1)}, u32[]{:S(2)}, u32[]{:S(2)}) %collective-permute-start.4) | collective-permute-done | bytes 393248 | tf_op jit(solution)/shard_map/ppermute | solution.py:447
  113.3 1.3 collective-permute-start.5
  114.6 1.5 collective-permute-start.6
  116.2 1.0 collective-permute-done.5.top_ref
  117.2 4.3 %collective-permute-done.6.bottom_ref = bf16[4,192,128]{2,1,0:T(8,128)(2,1)S(1)} collective-permute-done((bf16[4,192,128]{2,1,0:T(8,128)(2,1)S(1)}, bf16[4,192,128]{2,1,0:T(8,128)(2,1)S(1)}, u32[]{:S(2)}, u32[]{:S(2)}) %collective-permute-start.6) | collective-permute-done | bytes 196640 | tf_op jit(solution)/shard_map/ppermute | solution.py:381
  121.4 9.2 %shard_map.125 = (bf16[2,4,192,128]{3,2,1,0:T(8,128)(2,1)}, f32[8,16,64,128]{3,2,1,0:T(8,128)}) custom-call(f32[14]{0:T(128)S(1)} %pad_maximum_fusion.9.table_ref, bf16[2,4,192,128]{3,2,1,0:T(8,128)(2,1)S(1)} %copy-done.7, bf16[2,4,192,128]{3,2,1,0:T(8,128)(2,1)S(1)} %copy.83.prev_ref, bf16[4,192,128]{2,1,0:T(8,128)(2,1)S(1)} %collective-permute-done.5.top_ref, ...), custom_call_target="tpu_custom_call" | custom-call | flops 4076863488 | bytes 3956792 | tf_op jit(solution)/shard_map/pallas_call | solution.py:35
  130.7 1.9 collective-permute-start.7
  132.7 8.6 %collective-permute-done.7 = bf16[2,4,192,128]{3,2,0,1:T(8,128)(2,1)S(1)} collective-permute-done((bf16[2,4,192,128]{3,2,0,1:T(8,128)(2,1)S(1)}, bf16[2,4,192,128]{3,2,0,1:T(8,128)(2,1)S(1)}, u32[]{:S(2)}, u32[]{:S(2)}) %collective-permute-start.7) | collective-permute-done | bytes 393248 | tf_op jit(solution)/shard_map/ppermute | solution.py:452
  141.3 1.8 collective-permute-start.8
  143.1 1.1 convert.8
  144.2 28.0 %reduce-scatter.5.cloned.1.call-done = f32[1024,128]{1,0:T(8,128)} async-done(((f32[8192,128]{1,0:T(8,128)}), f32[1024,128]{1,0:T(8,128)}) %reduce-scatter.5.cloned.1.call-update) | async-done | bytes 524304 | tf_op jit(solution)/shard_map/reduce_scatter | solution.py:474
  172.2 1.1 convert.9
  174.1 6.7 %all-to-all-start.4 = ((bf16[16,128,128]{2,1,0:T(8,128)(2,1)}), bf16[16,128,128]{2,1,0:T(8,128)(2,1)}, u32[]{:S(2)}, u32[]{:S(2)}) async-start(bf16[16,128,128]{2,1,0:T(8,128)(2,1)} %pad_maximum_fusion), calls=%async_computation.6 | async-start | bytes 1048576 | tf_op jit(solution)/shard_map/all_to_all | solution.py:385
  180.9 1.3 collective-permute-start.9
  182.3 10.9 %collective-permute-done.9.bottom_ref = bf16[4,192,128]{2,1,0:T(8,128)(2,1)S(1)} collective-permute-done((bf16[4,192,128]{2,1,0:T(8,128)(2,1)S(1)}, bf16[4,192,128]{2,1,0:T(8,128)(2,1)S(1)}, u32[]{:S(2)}, u32[]{:S(2)}) %collective-permute-start.9) | collective-permute-done | bytes 196640 | tf_op jit(solution)/shard_map/ppermute | solution.py:381
  193.1 1.6 copy-done.12
  194.7 3.0 %shard_map.127.upstream_ref = f32[2,4,192,128]{3,2,1,0:T(8,128)S(1)} custom-call(f32[14]{0:T(128)S(1)} %pad_maximum_fusion.9.table_ref, bf16[2,4,192,128]{3,2,1,0:T(8,128)(2,1)S(1)} %shard_map.126.own_ref.grad_ref, bf16[2,4,192,128]{3,2,1,0:T(8,128)(2,1)S(1)} %copy.87.next_ref, bf16[4,192,128]{2,1,0:T(8,128)(2,1)S(1)} %collective-permute-done.8.top_ref, ...), custom_call_target="tpu_custom_call" | custom-call | flops 2038431744 | bytes 3170360 | tf_op jit(solution)/shard_map/pallas_call | solution.py:35
  197.8 1.9 shard_map.128
  199.7 5.0 %all-to-all-start.3 = ((f32[16,8,128]{2,1,0:T(8,128)}), f32[16,8,128]{2,1,0:T(8,128)S(1)}, u32[]{:S(2)}, u32[]{:S(2)}) async-start(f32[16,8,128]{2,1,0:T(8,128)} %get-tuple-element.29), calls=%async_computation.3 | async-start | bytes 131072 | tf_op jit(solution)/shard_map/all_to_all | solution.py:385
  204.7 1.1 convert_reduce_fusion
  205.9 5.4 %all-to-all-done.3.sums_ref = f32[16,8,128]{2,1,0:T(8,128)S(1)} async-done(((f32[16,8,128]{2,1,0:T(8,128)}), f32[16,8,128]{2,1,0:T(8,128)S(1)}, u32[]{:S(2)}, u32[]{:S(2)}) %all-to-all-start.3) | async-done | bytes 65568 | tf_op jit(solution)/shard_map/all_to_all | solution.py:385
  212.1 8.0 %all-to-all-start.5 = ((f32[8,128,128]{2,1,0:T(8,128)}), f32[8,128,128]{2,1,0:T(8,128)S(1)}, u32[]{:S(2)}, u32[]{:S(2)}) async-start(f32[8,128,128]{2,1,0:T(8,128)} %broadcast_in_dim.2), calls=%async_computation.7 | async-start | bytes 1048576 | tf_op jit(solution)/shard_map/all_to_all | solution.py:497
  220.1 1.3 shard_map.129
  221.4 8.1 %all-to-all-done.5 = f32[8,128,128]{2,1,0:T(8,128)S(1)} async-done(((f32[8,128,128]{2,1,0:T(8,128)}), f32[8,128,128]{2,1,0:T(8,128)S(1)}, u32[]{:S(2)}, u32[]{:S(2)}) %all-to-all-start.5) | async-done | bytes 524320 | tf_op jit(solution)/shard_map/all_to_all | solution.py:497
  (86 shorter events, 10.4 us)
Async XLA Ops:
  7.2 10.7 %copy-start = (bf16[2,4,192,128]{3,2,1,0:T(8,128)(2,1)S(1)}, bf16[2,4,192,128]{3,2,1,0:T(8,128)(2,1)}, u32[]{:S(2)}) copy-start(bf16[2,4,192,128]{3,2,1,0:T(8,128)(2,1)} %own_ref.7) | copy-start | bytes 1179652
  8.3 9.5 %collective-permute-start = (bf16[2,4,192,128]{3,2,0,1:T(8,128)(2,1)S(1)}, bf16[2,4,192,128]{3,2,0,1:T(8,128)(2,1)S(1)}, u32[]{:S(2)}, u32[]{:S(2)}) collective-permute-start(bf16[2,4,192,128]{3,2,0,1:T(8,128)(2,1)S(1)} %copy.71), channel_id=1, source_target_pairs={{0,16},{16,32},{32,48},{48,64},{64,80},{80,96},{96,112},{1,17},{17... | collective-permute-start | bytes 1179656 | tf_op jit(solution)/shard_map/ppermute | solution.py:416
  14.8 9.3 %collective-permute-start.1 = (bf16[2,4,192,128]{3,2,0,1:T(8,128)(2,1)}, bf16[2,4,192,128]{3,2,0,1:T(8,128)(2,1)S(1)}, u32[]{:S(2)}, u32[]{:S(2)}) collective-permute-start(bf16[2,4,192,128]{3,2,0,1:T(8,128)(2,1)} %get-tuple-element.69), channel_id=1, source_target_pairs={{16,0},{32,16},{48,32},{64,48},{80,64},{96,80},{112,96},{17,1},{33... | collective-permute-start | bytes 1179656 | tf_op jit(solution)/shard_map/ppermute | solution.py:417
  17.6 6.5 %copy-start.16 = (bf16[4,4,192,128]{3,2,0,1:T(8,128)(2,1)S(1)}, bf16[4,4,192,128]{3,2,0,1:T(8,128)(2,1)}, u32[]{:S(2)}) copy-start(bf16[4,4,192,128]{3,2,0,1:T(8,128)(2,1)} %get-tuple-element.70) | copy-start | bytes 2359300
  17.8 7.2 %copy-start.14 = (bf16[2,4,192,128]{3,2,0,1:T(8,128)(2,1)}, bf16[2,4,192,128]{3,2,0,1:T(8,128)(2,1)S(1)}, u32[]{:S(2)}) copy-start(bf16[2,4,192,128]{3,2,0,1:T(8,128)(2,1)S(1)} %collective-permute-done) | copy-start | bytes 1179652
  17.9 13.6 %copy-start.17 = (f32[192]{0:T(256)S(1)}, f32[192]{0:T(256)}, u32[]{:S(2)}) copy-start(f32[192]{0:T(256)} %param.15) | copy-start | bytes 2308
  17.9 13.6 %copy-start.18 = (f32[192]{0:T(256)S(1)}, f32[192]{0:T(256)}, u32[]{:S(2)}) copy-start(f32[192]{0:T(256)} %param.14) | copy-start | bytes 2308
  18.0 13.6 %copy-start.19 = (f32[192]{0:T(256)S(1)}, f32[192]{0:T(256)}, u32[]{:S(2)}) copy-start(f32[192]{0:T(256)} %param.13) | copy-start | bytes 2308
  18.0 13.6 %copy-start.20 = (f32[192]{0:T(256)S(1)}, f32[192]{0:T(256)}, u32[]{:S(2)}) copy-start(f32[192]{0:T(256)} %param.12) | copy-start | bytes 2308
  18.0 13.7 %copy-start.2 = (bf16[5184,192]{0,1:T(8,128)(2,1)S(1)}, bf16[5184,192]{0,1:T(8,128)(2,1)}, u32[]{:S(2)}) copy-start(bf16[5184,192]{0,1:T(8,128)(2,1)} %param.10) | copy-start | bytes 5971972
  25.0 32.4 %collective-permute-start.2 = (bf16[8,192,128]{2,1,0:T(8,128)(2,1)}, bf16[8,192,128]{2,1,0:T(8,128)(2,1)}, u32[]{:S(2)}, u32[]{:S(2)}) collective-permute-start(bf16[8,192,128]{2,1,0:T(8,128)(2,1)} %pad_maximum_fusion.1), channel_id=1, source_target_pairs={{0,1},{1,2},{2,3},{3,4},{4,5},{5,6},{6,7},{7,8},{8,9},{9,10},{10,1... | collective-permute-start | bytes 1179656 | tf_op jit(solution)/shard_map/ppermute | solution.py:381
  30.1 27.3 %collective-permute-start.3 = (bf16[8,192,128]{2,1,0:T(8,128)(2,1)}, bf16[8,192,128]{2,1,0:T(8,128)(2,1)}, u32[]{:S(2)}, u32[]{:S(2)}) collective-permute-start(bf16[8,192,128]{2,1,0:T(8,128)(2,1)} %pad_maximum_fusion.2), channel_id=1, source_target_pairs={{1,0},{2,1},{3,2},{4,3},{5,4},{6,5},{7,6},{8,7},{9,8},{10,9},{11,1... | collective-permute-start | bytes 1179656 | tf_op jit(solution)/shard_map/ppermute | solution.py:381
  31.7 1.6 copy-start.3
  33.2 7.5 %copy-start.15 = (bf16[2,4,192,128]{3,2,0,1:T(8,128)(2,1)S(1)}, bf16[2,4,192,128]{3,2,0,1:T(8,128)(2,1)}, u32[]{:S(2)}) copy-start(bf16[2,4,192,128]{3,2,0,1:T(8,128)(2,1)} %copy-done.14) | copy-start | bytes 1179652
  39.3 1.4 copy-start.11
  42.8 14.5 %all-to-all-start = ((f32[16,8,128]{2,1,0:T(8,128)}), f32[16,8,128]{2,1,0:T(8,128)S(1)}, u32[]{:S(2)}, u32[]{:S(2)}) async-start(f32[16,8,128]{2,1,0:T(8,128)} %shard_map.120), calls=%async_computation | async-start | bytes 131072 | tf_op jit(solution)/shard_map/all_to_all | solution.py:385
  51.7 17.9 %copy-start.5 = (bf16[2,4,192,128]{3,2,1,0:T(8,128)(2,1)S(1)}, bf16[2,4,192,128]{3,2,1,0:T(8,128)(2,1)}, u32[]{:S(2)}) copy-start(bf16[2,4,192,128]{3,2,1,0:T(8,128)(2,1)} %cot_ref.3) | copy-start | bytes 1179652
  65.0 0.9 copy-start.8
  65.8 10.0 %all-to-all-start.1 = ((f32[16,8,128]{2,1,0:T(8,128)}), f32[16,8,128]{2,1,0:T(8,128)S(1)}, u32[]{:S(2)}, u32[]{:S(2)}) async-start(f32[16,8,128]{2,1,0:T(8,128)} %get-tuple-element.20), calls=%async_computation.1 | async-start | bytes 131072 | tf_op jit(solution)/shard_map/all_to_all | solution.py:385
  69.3 73.8 %reduce-scatter.3.cloned.1.call-start = ((), (), s32[]{:S(2)}) async-start(), calls=%async_computation.8 | async-start | bytes 4718592 | tf_op jit(solution)/shard_map/reduce_scatter | solution.py:474
  69.6 1.0 copy-start.10
  70.6 1.6 copy-start.13
  72.2 3.7 %copy-start.9 = (f32[2,4,192,128]{3,2,1,0:T(8,128)S(1)}, f32[2,4,192,128]{3,2,1,0:T(8,128)}, u32[]{:S(2)}) copy-start(f32[2,4,192,128]{3,2,1,0:T(8,128)} %copy-done.8) | copy-start | bytes 2359300
  75.9 15.6 %copy-start.1 = (bf16[3456,512]{1,0:T(8,128)(2,1)S(1)}, bf16[3456,512]{1,0:T(8,128)(2,1)}, u32[]{:S(2)}) copy-start(bf16[3456,512]{1,0:T(8,128)(2,1)} %get-tuple-element.32.cols_ref) | copy-start | bytes 10616836
  77.2 0.8 copy-start.6
  98.2 23.2 %copy-start.4 = (bf16[5184,192]{0,1:T(8,128)(2,1)S(1)}, bf16[5184,192]{0,1:T(8,128)(2,1)}, u32[]{:S(2)}) copy-start(bf16[5184,192]{0,1:T(8,128)(2,1)} %param.11) | copy-start | bytes 5971972
  98.2 74.0 %reduce-scatter.5.cloned.1.call-start = ((), (), s32[]{:S(2)}) async-start(), calls=%async_computation.9 | async-start | bytes 4718592 | tf_op jit(solution)/shard_map/reduce_scatter | solution.py:474
  98.3 23.2 %copy-start.7 = (bf16[2,4,192,128]{3,2,1,0:T(8,128)(2,1)S(1)}, bf16[2,4,192,128]{3,2,1,0:T(8,128)(2,1)}, u32[]{:S(2)}) copy-start(bf16[2,4,192,128]{3,2,1,0:T(8,128)(2,1)} %copy-done.6) | copy-start | bytes 1179652
  99.4 13.8 %collective-permute-start.4 = (bf16[2,4,192,128]{3,2,0,1:T(8,128)(2,1)S(1)}, bf16[2,4,192,128]{3,2,0,1:T(8,128)(2,1)S(1)}, u32[]{:S(2)}, u32[]{:S(2)}) collective-permute-start(bf16[2,4,192,128]{3,2,0,1:T(8,128)(2,1)S(1)} %copy.80), channel_id=1, source_target_pairs={{0,16},{16,32},{32,48},{48,64},{64,80},{80,96},{96,112},{1,17},{17... | collective-permute-start | bytes 1179656 | tf_op jit(solution)/shard_map/ppermute | solution.py:447
  113.3 3.9 %collective-permute-start.5 = (bf16[4,192,128]{2,1,0:T(8,128)(2,1)S(1)}, bf16[4,192,128]{2,1,0:T(8,128)(2,1)S(1)}, u32[]{:S(2)}, u32[]{:S(2)}) collective-permute-start(bf16[4,192,128]{2,1,0:T(8,128)(2,1)S(1)} %pad_maximum_fusion.3), channel_id=1, source_target_pairs={{0,1},{1,2},{2,3},{3,4},{4,5},{5,6},{6,7},{7,8},{8,9},{9,10},{10,1... | collective-permute-start | bytes 589832 | tf_op jit(solution)/shard_map/ppermute | solution.py:381
  114.6 6.8 %collective-permute-start.6 = (bf16[4,192,128]{2,1,0:T(8,128)(2,1)S(1)}, bf16[4,192,128]{2,1,0:T(8,128)(2,1)S(1)}, u32[]{:S(2)}, u32[]{:S(2)}) collective-permute-start(bf16[4,192,128]{2,1,0:T(8,128)(2,1)S(1)} %pad_maximum_fusion.4), channel_id=1, source_target_pairs={{1,0},{2,1},{3,2},{4,3},{5,4},{6,5},{7,6},{8,7},{9,8},{10,9},{11,1... | collective-permute-start | bytes 589832 | tf_op jit(solution)/shard_map/ppermute | solution.py:381
  130.7 10.6 %collective-permute-start.7 = (bf16[2,4,192,128]{3,2,0,1:T(8,128)(2,1)S(1)}, bf16[2,4,192,128]{3,2,0,1:T(8,128)(2,1)S(1)}, u32[]{:S(2)}, u32[]{:S(2)}) collective-permute-start(bf16[2,4,192,128]{3,2,0,1:T(8,128)(2,1)S(1)} %copy.84), channel_id=1, source_target_pairs={{16,0},{32,16},{48,32},{64,48},{80,64},{96,80},{112,96},{17,1},{33... | collective-permute-start | bytes 1179656 | tf_op jit(solution)/shard_map/ppermute | solution.py:452
  141.3 40.9 %collective-permute-start.8 = (bf16[4,192,128]{2,1,0:T(8,128)(2,1)S(1)}, bf16[4,192,128]{2,1,0:T(8,128)(2,1)S(1)}, u32[]{:S(2)}, u32[]{:S(2)}) collective-permute-start(bf16[4,192,128]{2,1,0:T(8,128)(2,1)S(1)} %pad_maximum_fusion.5), channel_id=1, source_target_pairs={{0,1},{1,2},{2,3},{3,4},{4,5},{5,6},{6,7},{7,8},{8,9},{9,10},{10,1... | collective-permute-start | bytes 589832 | tf_op jit(solution)/shard_map/ppermute | solution.py:381
  174.1 25.6 %all-to-all-start.4 = ((bf16[16,128,128]{2,1,0:T(8,128)(2,1)}), bf16[16,128,128]{2,1,0:T(8,128)(2,1)}, u32[]{:S(2)}, u32[]{:S(2)}) async-start(bf16[16,128,128]{2,1,0:T(8,128)(2,1)} %pad_maximum_fusion), calls=%async_computation.6 | async-start | bytes 1048576 | tf_op jit(solution)/shard_map/all_to_all | solution.py:385
  180.9 12.2 %collective-permute-start.9 = (bf16[4,192,128]{2,1,0:T(8,128)(2,1)S(1)}, bf16[4,192,128]{2,1,0:T(8,128)(2,1)S(1)}, u32[]{:S(2)}, u32[]{:S(2)}) collective-permute-start(bf16[4,192,128]{2,1,0:T(8,128)(2,1)S(1)} %pad_maximum_fusion.6), channel_id=1, source_target_pairs={{1,0},{2,1},{3,2},{4,3},{5,4},{6,5},{7,6},{8,7},{9,8},{10,9},{11,1... | collective-permute-start | bytes 589832 | tf_op jit(solution)/shard_map/ppermute | solution.py:381
  193.1 1.6 copy-start.12
  199.7 11.6 %all-to-all-start.3 = ((f32[16,8,128]{2,1,0:T(8,128)}), f32[16,8,128]{2,1,0:T(8,128)S(1)}, u32[]{:S(2)}, u32[]{:S(2)}) async-start(f32[16,8,128]{2,1,0:T(8,128)} %get-tuple-element.29), calls=%async_computation.3 | async-start | bytes 131072 | tf_op jit(solution)/shard_map/all_to_all | solution.py:385
  212.1 17.5 %all-to-all-start.5 = ((f32[8,128,128]{2,1,0:T(8,128)}), f32[8,128,128]{2,1,0:T(8,128)S(1)}, u32[]{:S(2)}, u32[]{:S(2)}) async-start(f32[8,128,128]{2,1,0:T(8,128)} %broadcast_in_dim.2), calls=%async_computation.7 | async-start | bytes 1048576 | tf_op jit(solution)/shard_map/all_to_all | solution.py:497
Sparse Core Ops, SparseCore 0:
  98.3 36.2 reduce-scatter.2
  137.0 35.1 reduce-scatter.4

commit v2 on v1

v2 whole, which is shorter than its diff:
```python
import functools

import jax
import jax.numpy as jnp
from jax import lax
from jax.experimental import pallas as pl
from jax.experimental.pallas import tpu as pltpu
from jax.sharding import PartitionSpec as P

GROUPS = 32
NORM_EPSILON = 1e-05

C = 192
W = 128
PER_GROUP = C // GROUPS
ROWS = 4
OWN = 2
TAP_ROWS = 3 * C
DEPTH = 3 * TAP_ROWS
ALL_TAPS = 3 * DEPTH
SPACE = 16
TM = 8
SHARE = ALL_TAPS // SPACE
PACKED = 512
HALF = PACKED // 2
LOCAL_COUNT = ROWS * PER_GROUP * W
FULL_COUNT = LOCAL_COUNT * SPACE

F32 = jnp.float32
BF16 = jnp.bfloat16
EXACT = lax.Precision.HIGHEST


def call(kernel, out_shape, operands, smem=0, scratch=(), flops=0, **extra):
    nbytes = sum(x.size * x.dtype.itemsize for x in operands)
    return pl.pallas_call(
        kernel,
        out_shape=out_shape,
        in_specs=[pl.BlockSpec(memory_space=pltpu.SMEM)] * smem
        + [pl.BlockSpec(memory_space=pltpu.VMEM)] * (len(operands) - smem),
        out_specs=jax.tree.map(lambda _: pl.BlockSpec(memory_space=pltpu.VMEM), out_shape),
        scratch_shapes=list(scratch),
        compiler_params=pltpu.CompilerParams(vmem_limit_bytes=48 * 1024 * 1024),
        cost_estimate=pl.CostEstimate(flops=flops, bytes_accessed=nbytes, transcendentals=0),
        **extra,
    )(*operands)


def lane_ids(rows=C):
    return lax.broadcasted_iota(jnp.int32, (rows, W), 1)


def membership():
    channel = lax.broadcasted_iota(jnp.int32, (C, W), 0)
    group = lane_ids()
    inside = (channel >= group * PER_GROUP) & (channel < (group + 1) * PER_GROUP)
    return inside.astype(F32)


def to_groups(columns):
    lanes = lane_ids()
    packed = jnp.zeros((C, W), F32)
    for i, column in enumerate(columns):
        packed = jnp.where(lanes == i, column, packed)
    summed = lax.dot_general(
        packed, membership(), (((0,), (0,)), ((), ())), precision=EXACT, preferred_element_type=F32
    )
    return summed[:8]


def to_channels(table):
    return lax.dot_general(
        membership(), table, (((1,), (1,)), ((), ())), precision=EXACT, preferred_element_type=F32
    )


def merged_stats(parts_ref):
    means = parts_ref[:, 0:4, :]
    mean = jnp.sum(means, axis=0) * (1.0 / SPACE)
    spread = jnp.sum((means - mean[None]) ** 2, axis=0) * float(LOCAL_COUNT)
    variance = (jnp.sum(parts_ref[:, 4:8, :], axis=0) + spread) * (1.0 / FULL_COUNT)
    inverse = lax.rsqrt(variance + NORM_EPSILON)
    return to_channels(jnp.concatenate([mean, inverse], axis=0))


def local_stats(blocks):
    sums = []
    for rows in blocks:
        total = rows[0]()
        for row in rows[1:]:
            total = total + row()
        sums.append(jnp.sum(total, axis=1, keepdims=True))
    means = to_groups(sums) * (1.0 / LOCAL_COUNT)
    spread = to_channels(means)
    squares = []
    for f, rows in enumerate(blocks):
        total = None
        for row in rows:
            centered = row() - spread[:, f : f + 1]
            total = centered * centered if total is None else total + centered * centered
        squares.append(jnp.sum(total, axis=1, keepdims=True))
    deviations = to_groups(squares)
    return jnp.concatenate([means[:4], deviations[:4]], axis=0)


def store_shifted(cols_ref, h, f, field):
    lanes = lane_ids()
    before = jnp.where(lanes == 0, 0.0, pltpu.roll(field, 1, 1))
    after = jnp.where(lanes == W - 1, 0.0, pltpu.roll(field, W - 1, 1))
    for s, part in enumerate((before, field, after)):
        start = h * TAP_ROWS + s * C
        cols_ref[start : start + C, f * W : (f + 1) * W] = part.astype(BF16)


def conv_rows(kernels, cols_ref, factors, finish):
    wide = lax.broadcasted_iota(jnp.int32, (C, 2 * W), 1) < W
    for h in range(ROWS):
        total = None
        for k in range(3):
            part = jnp.dot(
                kernels[k],
                cols_ref[h * TAP_ROWS : h * TAP_ROWS + DEPTH, k * W : (k + 2) * W],
                preferred_element_type=F32,
            )
            if factors[k] is not None:
                part = part * jnp.where(wide, factors[k][0], factors[k][1])
            total = part if total is None else total + part
        finish(h, total)


def edges_kernel(*refs, count):
    low_ref, high_ref = refs[count:]
    for i, ref in enumerate(refs[:count]):
        for f in range(OWN):
            low_ref[i * OWN + f] = ref[f, ROWS - 1]
            high_ref[i * OWN + f] = ref[f, 0]


def stats_kernel(own_ref, out_ref):
    def row(f, h):
        return lambda: own_ref[f, h].astype(F32)

    blocks = [[row(f, h) for h in range(ROWS)] for f in range(OWN)]
    out_ref[...] = jnp.broadcast_to(local_stats(blocks)[None], (SPACE, 8, W))


def silu_of(pre):
    return pre / (1.0 + jnp.exp(-pre))


def active_columns(cols_ref, table_ref, own_stats, prev_stats, gain, bias, own, prev, above, below):
    shift = jnp.broadcast_to(bias, (C, W))
    for f in range(4):
        stats = prev_stats if f < OWN else own_stats
        g = f % OWN
        mean = jnp.broadcast_to(stats[:, g : g + 1], (C, W))
        scale = jnp.broadcast_to(stats[:, 4 + g : 5 + g] * gain, (C, W))
        for h in range(ROWS + 2):
            if h == 0:
                field = above[f]
            elif h == ROWS + 1:
                field = below[f]
            else:
                field = (prev if f < OWN else own)[g, h - 1]
            active = silu_of((field.astype(F32) - mean) * scale + shift)
            if h == 0:
                active = active * table_ref[12]
            if h == ROWS + 1:
                active = active * table_ref[13]
            store_shifted(cols_ref, h, f, active)


def forward_conv(table_ref, weight_ref, cols_ref, finish):
    kernels = [weight_ref[:, k * DEPTH : (k + 1) * DEPTH] for k in range(3)]
    factors = [(table_ref[(2 - k) * 4], table_ref[(2 - k) * 4 + 1]) for k in range(2)] + [None]
    conv_rows(kernels, cols_ref, factors, finish)


def conv_one_kernel(
    table_ref, parts_ref, prev_parts_ref, own_ref, prev_ref, above_ref, below_ref, param_ref, weight_ref,
    cols_ref, conv_ref, half_ref, out_ref,
):
    active_columns(
        cols_ref, table_ref, merged_stats(parts_ref), merged_stats(prev_parts_ref),
        param_ref[:, 0:1], param_ref[:, 1:2], own_ref, prev_ref, above_ref, below_ref,
    )

    def finish(h, total):
        for f in range(OWN):
            field = total[:, f * W : (f + 1) * W]
            conv_ref[f, h] = field
            half_ref[f, h] = field.astype(BF16)

    forward_conv(table_ref, weight_ref, cols_ref, finish)

    def row(f, h):
        return lambda: conv_ref[f, h]

    blocks = [[row(f, h) for h in range(ROWS)] for f in range(OWN)]
    out_ref[...] = jnp.broadcast_to(local_stats(blocks)[None], (SPACE, 8, W))


def turn_kernel(src_ref, dst_ref):
    row = lax.broadcasted_iota(jnp.int32, (C, C), 0)
    eye = (row == lax.broadcasted_iota(jnp.int32, (C, C), 1)).astype(BF16)
    for tap in range(27):
        k, spot = divmod(26 - tap, 9)
        block = lax.dot_general(
            eye, src_ref[:, tap * C : (tap + 1) * C], (((1,), (1,)), ((), ())), preferred_element_type=F32
        )
        dst_ref[k, :, spot * C : (spot + 1) * C] = block.astype(BF16)


def adjoint_kernel(table_ref, own_ref, next_ref, above_ref, below_ref, weight_ref, out_ref, cols_ref, *, first):
    for f in range(4):
        for h in range(ROWS + 2):
            if h == 0:
                field = above_ref[first + f]
            elif h == ROWS + 1:
                field = below_ref[first + f]
            else:
                field = (own_ref if f < OWN else next_ref)[f % OWN, h - 1]
            store_shifted(cols_ref, h, f, field.astype(F32))
    factors = [None] + [(table_ref[j * 4 + j], table_ref[j * 4 + j + 1]) for j in (1, 2)]

    def finish(h, total):
        out_ref[0, h] = total[:, :W]
        out_ref[1, h] = total[:, W:]

    conv_rows([weight_ref[j] for j in range(3)], cols_ref, factors, finish)


def norm_grad_kernel(parts_ref, field_ref, upstream_ref, param_ref, grad_ref, norm_ref, out_ref, *, place):
    stats = merged_stats(parts_ref)
    gain = jnp.broadcast_to(param_ref[:, place : place + 1], (C, W))
    bias = jnp.broadcast_to(param_ref[:, place + 1 : place + 2], (C, W))
    plain, weighted = [], []
    for f in range(OWN):
        mean = jnp.broadcast_to(stats[:, f : f + 1], (C, W))
        inverse = jnp.broadcast_to(stats[:, 4 + f : 5 + f], (C, W))
        sums = None
        for h in range(ROWS):
            normalized = (field_ref[f, h].astype(F32) - mean) * inverse
            pre = normalized * gain + bias
            sigmoid = 1.0 / (1.0 + jnp.exp(-pre))
            grad = upstream_ref[f, h] * (sigmoid * (1.0 + pre * (1.0 - sigmoid))) * gain
            grad_ref[f, h] = grad
            norm_ref[f, h] = normalized
            pair = (grad, grad * normalized)
            sums = pair if sums is None else (sums[0] + pair[0], sums[1] + pair[1])
        plain.append(jnp.sum(sums[0], axis=1, keepdims=True))
        weighted.append(jnp.sum(sums[1], axis=1, keepdims=True))
    out_ref[...] = jnp.broadcast_to(to_groups(plain + weighted)[None], (SPACE, 8, W))


def field_grad(parts_ref, sums_ref, grad_ref, norm_ref, finish):
    stats = merged_stats(parts_ref)
    totals = to_channels(jnp.sum(sums_ref[...], axis=0) * (1.0 / FULL_COUNT))
    for f in range(OWN):
        inverse = jnp.broadcast_to(stats[:, 4 + f : 5 + f], (C, W))
        plain = jnp.broadcast_to(totals[:, f : f + 1], (C, W))
        weighted = jnp.broadcast_to(totals[:, OWN + f : OWN + f + 1], (C, W))
        for h in range(ROWS):
            finish(f, h, inverse * (grad_ref[f, h] - plain - norm_ref[f, h] * weighted))


def grad_conv_kernel(parts_ref, sums_ref, grad_ref, norm_ref, out_ref):
    def finish(f, h, value):
        out_ref[f, h] = value.astype(BF16)

    field_grad(parts_ref, sums_ref, grad_ref, norm_ref, finish)


def input_grad_kernel(parts_ref, sums_ref, grad_ref, norm_ref, cot_ref, out_ref):
    def finish(f, h, value):
        out_ref[f, h] = (cot_ref[f, h].astype(F32) + value).astype(BF16)

    field_grad(parts_ref, sums_ref, grad_ref, norm_ref, finish)


def weight_grad(table_ref, core_ref, cols_ref, grad_ref, kept_ref, send_ref, dense_ref, turned_ref):
    for h in range(ROWS):
        for f in range(OWN):
            block = grad_ref[f, h].T
            start = (h * OWN + f) * W
            turned_ref[2, start : start + W, :] = block
            wide = block.astype(F32)
            for k in range(2):
                turned_ref[k, start : start + W, :] = (wide * table_ref[(2 - k) * 4 + f]).astype(BF16)
    for k in range(3):
        for spot in range(9):
            start = spot * C
            rows = [
                cols_ref[h * TAP_ROWS + start : h * TAP_ROWS + start + C, k * W : (k + 2) * W]
                for h in range(ROWS)
            ]
            dense_ref[k * DEPTH + start : k * DEPTH + start + C, :] = jnp.dot(
                jnp.concatenate(rows, axis=1), turned_ref[k], preferred_element_type=F32
            )
    half = SHARE // 2
    first = core_ref[0] == 0
    for s in range(SPACE):
        low = dense_ref[s * SHARE : (s + 1) * SHARE, 0:W]
        high = jnp.concatenate(
            [
                dense_ref[s * SHARE : s * SHARE + half, W:C],
                dense_ref[s * SHARE + half : (s + 1) * SHARE, W:C],
            ],
            axis=1,
        )
        spare = jnp.zeros((PACKED - SHARE - half, W), F32)
        packed = jnp.concatenate([low, high, spare], axis=0).astype(BF16)
        kept_ref[s] = jnp.where(first, packed[:HALF], packed[HALF:])
        send_ref[s] = jnp.where(first, packed[HALF:], packed[:HALF])


def weight_one_kernel(table_ref, core_ref, cols_ref, grad_ref, kept_ref, send_ref, dense_ref, turned_ref):
    weight_grad(table_ref, core_ref, cols_ref, grad_ref, kept_ref, send_ref, dense_ref, turned_ref)


def conv_two_kernel(
    table_ref, core_ref, parts_ref, prev_parts_ref, own_ref, prev_ref, above_ref, below_ref, param_ref, weight_ref,
    input_ref, cot_ref, decoded_ref, kept_ref, send_ref, cols_ref, dense_ref, turned_ref,
):
    active_columns(
        cols_ref, table_ref, merged_stats(parts_ref), merged_stats(prev_parts_ref),
        param_ref[:, 2:3], param_ref[:, 3:4], own_ref, prev_ref, above_ref, below_ref,
    )

    def finish(h, total):
        for f in range(OWN):
            field = input_ref[f, h].astype(F32) + total[:, f * W : (f + 1) * W]
            decoded_ref[f, h] = field.astype(BF16)

    forward_conv(table_ref, weight_ref, cols_ref, finish)
    weight_grad(table_ref, core_ref, cols_ref, cot_ref, kept_ref, send_ref, dense_ref, turned_ref)


def add_kernel(kept_ref, came_ref, out_ref):
    out_ref[...] = (kept_ref[...].astype(F32) + came_ref[...].astype(F32)).astype(BF16)


def gather_kernel(parts_ref, out_ref):
    total = parts_ref[0].astype(F32)
    for s in range(1, SPACE):
        total = total + parts_ref[s].astype(F32)
    total = total.astype(BF16)
    for i in range(TM):
        out_ref[i] = total


def unpack_kernel(parts_ref, out_ref, *, scale):
    halves = []
    for core in range(2):
        total = parts_ref[core].astype(F32)
        for i in range(2 + core, TM, 2):
            total = total + parts_ref[i].astype(F32)
        halves.append(total * scale)
    packed = jnp.concatenate(halves, axis=0)
    half = SHARE // 2
    low = packed[0:SHARE]
    high = packed[SHARE : SHARE + half]
    out_ref[0:W, :] = low.T
    out_ref[W:C, 0:half] = high[:, : C - W].T
    out_ref[W:C, half:SHARE] = high[:, C - W :].T


def keep_table(first_frame, frame_count, clip_ends):
    frame_ids = first_frame + jnp.arange(frame_count, dtype=jnp.int32)
    own_clip = jnp.sum((frame_ids[:, None] >= clip_ends[None, :]).astype(jnp.int32), axis=1)
    lagged = [jnp.ones((frame_count,), F32)]
    for lag_size in (1, 2):
        shifted_ids = frame_ids - lag_size
        before_clip = jnp.sum((shifted_ids[:, None] >= clip_ends[None, :]).astype(jnp.int32), axis=1)
        allowed = (shifted_ids >= 0) & (before_clip == own_clip)
        lagged.append(allowed.astype(F32))
    return jnp.stack(lagged)


FORWARD = [(i, i + 1) for i in range(TM - 1)]
BACKWARD = [(i + 1, i) for i in range(TM - 1)]
DOWN = [(i, i + 1) for i in range(SPACE - 1)]
UP = [(i + 1, i) for i in range(SPACE - 1)]


SIBLING = [(i, i ^ 1) for i in range(TM)]


def row_halos(*blocks):
    rows = shape((OWN * len(blocks), C, W), BF16)
    low, high = call(functools.partial(edges_kernel, count=len(blocks)), (rows, rows), blocks)
    return lax.ppermute(low, "space", DOWN), lax.ppermute(high, "space", UP)


def swap(parts):
    return lax.all_to_all(parts, "space", 0, 0)


def shape(dims, dtype=F32):
    return jax.ShapeDtypeStruct(dims, dtype)


CONV_FLOPS = 2 * OWN * ROWS * W * ALL_TAPS * C
FIELD = (OWN, ROWS, C, W)
COLS = (6 * TAP_ROWS, 4 * W)


def shards(
    activations,
    weight_one,
    weight_two,
    gain_one,
    bias_one,
    gain_two,
    bias_two,
    cotangent,
    clip_lengths,
):
    clip_ends = jnp.cumsum(clip_lengths)
    row = lax.axis_index("space")
    keeps = keep_table(lax.axis_index("tm") * OWN, 4, clip_ends)
    edges = jnp.stack([row > 0, row < SPACE - 1]).astype(F32)
    table = jnp.concatenate([keeps.reshape(-1), edges])
    core = (lax.axis_index("tm") % 2).astype(jnp.int32).reshape(1)
    params = jnp.stack([gain_one, bias_one, gain_two, bias_two], axis=1)
    turned_one, turned_two = weight_one.T, weight_two.T
    payload = shape((SPACE, 8, W))

    previous = lax.ppermute(activations, "tm", FORWARD)
    following = lax.ppermute(cotangent, "tm", BACKWARD)
    stats_one = swap(call(stats_kernel, payload, (activations,)))
    above, below = row_halos(previous, activations, cotangent, following)
    earlier_one = lax.ppermute(stats_one, "tm", FORWARD)
    adjoint_two = call(turn_kernel, shape((3, C, DEPTH), BF16), (turned_two,))
    columns_one, conv_one, half_one, parts = call(
        conv_one_kernel,
        (shape(COLS, BF16), shape(FIELD), shape(FIELD, BF16), payload),
        (table, stats_one, earlier_one, activations, previous, above, below, params, turned_one),
        smem=1,
        flops=CONV_FLOPS,
    )
    stats_two = swap(parts)
    previous_two = lax.ppermute(half_one, "tm", FORWARD)
    above_two, below_two = row_halos(previous_two, half_one)
    grad_active_two = call(
        functools.partial(adjoint_kernel, first=4),
        shape(FIELD),
        (table, cotangent, following, above, below, adjoint_two),
        smem=1,
        scratch=[pltpu.VMEM(COLS, BF16)],
        flops=CONV_FLOPS,
    )
    earlier_two = lax.ppermute(stats_two, "tm", FORWARD)
    grad_norm, normalized, parts = call(
        functools.partial(norm_grad_kernel, place=2),
        (shape(FIELD), shape(FIELD), payload),
        (stats_two, conv_one, grad_active_two, params),
    )
    sums_two = swap(parts)
    packed = shape((SPACE, HALF, W), BF16)
    dense = [pltpu.VMEM((ALL_TAPS, C), F32), pltpu.VMEM((3, OWN * ROWS * W, C), BF16)]
    decoded, kept_two, sent_two = call(
        conv_two_kernel,
        (shape(FIELD, BF16), packed, packed),
        (
            table, core, stats_two, earlier_two, conv_one, previous_two, above_two, below_two, params, turned_two,
            activations, cotangent,
        ),
        smem=2,
        scratch=[pltpu.VMEM(COLS, BF16)] + dense,
        flops=2 * CONV_FLOPS,
    )
    grad_conv_one = call(
        grad_conv_kernel, shape(FIELD, BF16), (stats_two, sums_two, grad_norm, normalized)
    )
    following_one = lax.ppermute(grad_conv_one, "tm", BACKWARD)
    kept_one, sent_one = call(
        weight_one_kernel,
        (packed, packed),
        (table, core, columns_one, grad_conv_one),
        smem=2,
        scratch=dense,
        flops=CONV_FLOPS,
    )
    above_one, below_one = row_halos(grad_conv_one, following_one)
    adjoint_one = call(turn_kernel, shape((3, C, DEPTH), BF16), (turned_one,))
    grad_active_one = call(
        functools.partial(adjoint_kernel, first=0),
        shape(FIELD),
        (table, grad_conv_one, following_one, above_one, below_one, adjoint_one),
        smem=1,
        scratch=[pltpu.VMEM(COLS, BF16)],
        flops=CONV_FLOPS,
    )
    grad_norm, normalized, parts = call(
        functools.partial(norm_grad_kernel, place=0),
        (shape(FIELD), shape(FIELD), payload),
        (stats_one, activations, grad_active_one, params),
    )
    sums_one = swap(parts)
    input_grad = call(
        input_grad_kernel, shape(FIELD, BF16), (stats_one, sums_one, grad_norm, normalized, cotangent)
    )
    total_cells = OWN * TM * ROWS * SPACE * W
    shares = []
    for kept, sent in ((kept_one, sent_one), (kept_two, sent_two)):
        pair = call(add_kernel, packed, (kept, lax.ppermute(sent, "tm", SIBLING)))
        spread = call(gather_kernel, shape((TM, HALF, W), BF16), (swap(pair),))
        share = call(
            functools.partial(unpack_kernel, scale=float(total_cells) ** -0.5),
            shape((C, SHARE)),
            (lax.all_to_all(spread, "tm", 0, 0),),
        )
        shares.append(share.T)
    return (decoded, input_grad, shares[0], shares[1])


def solution(mesh):
    placed = (
        P("tm", "space", None, None),
        P(),
        P(),
        P(),
        P(),
        P(),
        P(),
        P("tm", "space", None, None),
        P(),
    )
    return jax.shard_map(
        shards,
        mesh=mesh,
        in_specs=placed,
        out_specs=(
            P("tm", "space", None, None),
            P("tm", "space", None, None),
            P("space", None),
            P("space", None),
        ),
        check_vma=False,
    )
```

time: 240 us -> 214 us (0.89)
  waiting for transfers between devices: 85.2 us -> 47.7 us
  starting transfers between devices: 57.1 us -> 89.3 us
  between operations: 14.6 us -> 1.12 us
  blocking collectives: 12.9 us -> 0 us
  local copies, waits for them, and re-layouts: 17.9 us -> 25.1 us
  other arithmetic: 7.07 us -> 1.3 us
  Pallas kernels: 43.6 us -> 47.7 us
    reduce_scatter x2 -> x0, waiting for transfers between devices: 28 us -> none  [shards(): lax.psum_scatter(local.reshape(TM * rows, W), 'tm', scatter_dimension=0,...]
    all_to_all x4 -> x6, waiting for transfers between devices: 11.1 us -> 31.5 us  [swap(): return lax.all_to_all(parts, 'space', 0, 0)]
    all_to_all x4 -> x6, starting transfers between devices: 23.3 us -> 38.6 us  [swap(): return lax.all_to_all(parts, 'space', 0, 0)]
    ppermute x6, waiting for transfers between devices: 16.1 us -> 1.51 us  [row_halos(): return (lax.ppermute(low, 'space', DOWN), lax.ppermute(high, 'space', UP))]
    all_to_all x1 -> x0, blocking collectives: 12.9 us -> none  [swap(): return lax.all_to_all(parts, 'space', 0, 0)]
    unnamed x47 -> x68, local copies, waits for them, and re-layouts: 13.6 us -> 24.9 us
    ppermute x1 -> x5, starting transfers between devices: 5.73 us -> 16.3 us  [the longest x1 5.28 us: shards(): previous_two = lax.ppermute(half_one, 'tm', FORWARD)]
    ppermute x1, waiting for transfers between devices: 8.64 us -> 0.01 us  [shards(): following_one = lax.ppermute(grad_conv_one, 'tm', BACKWARD)]
  transfers between devices with their start and end apart: 17 -> 22, of which waited for: 10 -> 8; matrix products, arithmetic and copies ran while one was open for 5% -> 1% of each run, Pallas kernels for 11% -> 18%
where the time goes in v2:
time: 214 us; the launch traced here: 212 us
  starting transfers between devices  89.3 us (42%)
  Pallas kernels  47.7 us (22%)
  waiting for transfers between devices  47.7 us (22%)
  local copies, waits for them, and re-layouts  25.1 us (12%)
    pallas_call x21, Pallas kernels, call(): pl.pallas_call(kernel, out_shape=out_shape, in_specs=[pl.BlockSpec(memory...  47.7 us
    all_to_all x6, starting transfers between devices, swap(): return lax.all_to_all(parts, 'space', 0, 0)  38.6 us
    all_to_all x6, waiting for transfers between devices, swap(): return lax.all_to_all(parts, 'space', 0, 0)  31.5 us
    unnamed x68, local copies, waits for them, and re-layouts  24.9 us
    ppermute x6, starting transfers between devices, row_halos(): return (lax.ppermute(low, 'space', DOWN), lax.ppermute(high, 'space', UP))  13.8 us
    all_to_all x2, waiting for transfers between devices, shards(): lax.all_to_all(spread, 'tm', 0, 0)  13.4 us
    all_to_all x2, starting transfers between devices, shards(): lax.all_to_all(spread, 'tm', 0, 0)  12.3 us
    ppermute x1, starting transfers between devices, shards(): previous_two = lax.ppermute(half_one, 'tm', FORWARD)  5.28 us
  transfers between devices with their start and end apart: 22, of which 8 were waited for; matrix products, arithmetic and copies ran while one was open for 1% of the time, Pallas kernels for 18%

profile of v2, /device:TPU:1, one launch (start us, length us, event | category | flops | bytes accessed | tf_op | source)
XLA Modules:
  0.0 212.2 jit_solution(12585475018654491703)
XLA Ops:
  0.6 4.5 %collective-permute-start.1 = (bf16[2,4,192,128]{3,2,1,0:T(8,128)(2,1)}, bf16[2,4,192,128]{3,2,1,0:T(8,128)(2,1)S(1)}, u32[]{:S(2)}, u32[]{:S(2)}) collective-permute-start(bf16[2,4,192,128]{3,2,1,0:T(8,128)(2,1)} %field_ref.1), channel_id=1, source_target_pairs={{0,16},{16,32},{32,48},{48,64},{64,80},{80,96},{96,112},{1,17},{17... | collective-permute-start | bytes 1179656 | tf_op jit(solution)/shard_map/ppermute | solution.py:429
  5.2 1.9 collective-permute-start.2
  8.1 1.9 shard_map.120
  10.0 7.8 %all-to-all-start = ((f32[16,8,128]{2,1,0:T(8,128)}), f32[16,8,128]{2,1,0:T(8,128)S(1)}, u32[]{:S(2)}, u32[]{:S(2)}) async-start(f32[16,8,128]{2,1,0:T(8,128)} %shard_map.120), calls=%async_computation | async-start | bytes 131072 | tf_op jit(solution)/shard_map/all_to_all | solution.py:396
  18.9 1.1 copy-done.1
  22.0 3.3 %collective-permute-start.3 = (bf16[8,192,128]{2,1,0:T(8,128)(2,1)}, bf16[8,192,128]{2,1,0:T(8,128)(2,1)S(1)}, u32[]{:S(2)}, u32[]{:S(2)}) collective-permute-start(bf16[8,192,128]{2,1,0:T(8,128)(2,1)} %get-tuple-element.25), channel_id=1, source_target_pairs={{0,1},{1,2},{2,3},{3,4},{4,5},{5,6},{6,7},{7,8},{8,9},{9,10},{10,1... | collective-permute-start | bytes 1179656 | tf_op jit(solution)/shard_map/ppermute | solution.py:392
  25.3 1.3 collective-permute-start.4
  27.0 1.6 copy-done.5
  29.7 4.5 %collective-permute-start = (f32[16,8,128]{2,1,0:T(8,128)S(1)}, f32[16,8,128]{2,1,0:T(8,128)S(1)}, u32[]{:S(2)}, u32[]{:S(2)}) collective-permute-start(f32[16,8,128]{2,1,0:T(8,128)S(1)} %all-to-all-done.parts_ref), channel_id=1, source_target_pairs={{0,16},{16,32},{32,48},{48,64},{64,80},{80,96},{96,112},{1,17},{17... | collective-permute-start | bytes 196616 | tf_op jit(solution)/shard_map/ppermute | solution.py:433
  34.2 1.2 collective-permute-done.prev_parts_ref
  36.2 1.5 collective-permute-done.4.below_ref
  38.4 1.6 copy-done.3
  43.0 7.0 %shard_map.122 = (bf16[3456,512]{1,0:T(8,128)(2,1)}, f32[2,4,192,128]{3,2,1,0:T(8,128)S(1)}, bf16[2,4,192,128]{3,2,1,0:T(8,128)(2,1)S(1)}, f32[16,8,128]{2,1,0:T(8,128)}) custom-call(f32[14]{0:T(128)S(1)} %pad_maximum_fusion.2.table_ref, f32[16,8,128]{2,1,0:T(8,128)S(1)} %all-to-all-done.parts_ref, f32[16,8,128]{2,1,0:T(8,128)S(1)} %collective-permute-done.prev_parts_ref, ...), custom_call_target="tpu_custom_call" | custom-call | flops 2038431744 | bytes 3697720 | tf_op jit(solution)/shard_map/pallas_call | solution.py:36
  50.9 8.0 %all-to-all-start.1 = ((f32[16,8,128]{2,1,0:T(8,128)}), f32[16,8,128]{2,1,0:T(8,128)S(1)}, u32[]{:S(2)}, u32[]{:S(2)}) async-start(f32[16,8,128]{2,1,0:T(8,128)} %get-tuple-element.27), calls=%async_computation.1 | async-start | bytes 131072 | tf_op jit(solution)/shard_map/all_to_all | solution.py:396
  61.9 3.0 %shard_map.126.upstream_ref = f32[2,4,192,128]{3,2,1,0:T(8,128)S(1)} custom-call(f32[14]{0:T(128)S(1)} %pad_maximum_fusion.2.table_ref, bf16[2,4,192,128]{3,2,1,0:T(8,128)(2,1)S(1)} %copy-done.7, bf16[2,4,192,128]{3,2,1,0:T(8,128)(2,1)S(1)} %copy-done.20, bf16[8,192,128]{2,1,0:T(8,128)(2,1)S(1)} %copy-done.25, bf16[8,192,128]{2,1,0:T(8,128)(2,1)S(1)} %copy-done.28, ...), custom_call_target="tpu_custom_call" | custom-call | flops 2038431744 | bytes 3563576 | tf_op jit(solution)/shard_map/pallas_call | solution.py:36
  65.8 1.1 copy-done.15
  67.0 1.1 copy-done.18
  68.1 1.9 shard_map.127
  70.0 6.7 %all-to-all-start.2 = ((f32[16,8,128]{2,1,0:T(8,128)}), f32[16,8,128]{2,1,0:T(8,128)S(1)}, u32[]{:S(2)}, u32[]{:S(2)}) async-start(f32[16,8,128]{2,1,0:T(8,128)} %get-tuple-element.33), calls=%async_computation.2 | async-start | bytes 131072 | tf_op jit(solution)/shard_map/all_to_all | solution.py:396
  76.6 5.3 %collective-permute-start.6 = (bf16[2,4,192,128]{3,2,1,0:T(8,128)(2,1)S(1)}, bf16[2,4,192,128]{3,2,1,0:T(8,128)(2,1)}, u32[]{:S(2)}, u32[]{:S(2)}) collective-permute-start(bf16[2,4,192,128]{3,2,1,0:T(8,128)(2,1)S(1)} %get-tuple-element.29.refs_1_), channel_id=1, source_target_pairs={{0,16},{16,32},{32,48},{48,64},{64,80},{80,96},{96,112},{1,17},{17... | collective-permute-start | bytes 1179656 | tf_op jit(solution)/shard_map/ppermute | solution.py:443
  81.9 1.2 all-to-all-done.2.sums_ref
  83.7 2.0 copy-done.29
  85.7 4.9 %shard_map.134 = (bf16[16,256,128]{2,1,0:T(8,128)(2,1)S(1)}, bf16[16,256,128]{2,1,0:T(8,128)(2,1)}) custom-call(f32[14]{0:T(128)S(1)} %pad_maximum_fusion.2.table_ref, s32[1]{0:T(128)} %bitcast.6.core_ref, bf16[3456,512]{1,0:T(8,128)(2,1)S(1)} %copy-done.29, bf16[2,4,192,128]{3,2,1,0:T(8,128)(2,1)S(1)} %shard_map.128.refs_0_.own_ref.grad_ref), custom_call_target="tpu_custom_call" | custom-call | flops 2038431744 | bytes 3932220 | tf_op jit(solution)/shard_map/pallas_call | solution.py:36
  90.6 2.1 %collective-permute-start.12 = (bf16[16,256,128]{2,1,0:T(8,128)(2,1)}, bf16[16,256,128]{2,1,0:T(8,128)(2,1)}, u32[]{:S(2)}, u32[]{:S(2)}) collective-permute-start(bf16[16,256,128]{2,1,0:T(8,128)(2,1)} %get-tuple-element.43), channel_id=1, source_target_pairs={{0,16},{16,0},{32,48},{48,32},{64,80},{80,64},{96,112},{112,96},{1... | collective-permute-start | bytes 3145736 | tf_op jit(solution)/shard_map/ppermute | solution.py:507
  92.7 1.9 collective-permute-start.9
  95.7 2.2 %collective-permute-start.7 = (bf16[4,192,128]{2,1,0:T(8,128)(2,1)S(1)}, bf16[4,192,128]{2,1,0:T(8,128)(2,1)S(1)}, u32[]{:S(2)}, u32[]{:S(2)}) collective-permute-start(bf16[4,192,128]{2,1,0:T(8,128)(2,1)S(1)} %get-tuple-element.30), channel_id=1, source_target_pairs={{0,1},{1,2},{2,3},{3,4},{4,5},{5,6},{6,7},{7,8},{8,9},{9,10},{10,1... | collective-permute-start | bytes 589832 | tf_op jit(solution)/shard_map/ppermute | solution.py:392
  97.9 1.4 collective-permute-start.8
  99.3 4.4 %collective-permute-start.5 = (f32[16,8,128]{2,1,0:T(8,128)S(1)}, f32[16,8,128]{2,1,0:T(8,128)S(1)}, u32[]{:S(2)}, u32[]{:S(2)}) collective-permute-start(f32[16,8,128]{2,1,0:T(8,128)S(1)} %all-to-all-done.1.parts_ref), channel_id=1, source_target_pairs={{0,16},{16,32},{32,48},{48,64},{64,80},{80,96},{96,112},{1,17},{17... | collective-permute-start | bytes 196616 | tf_op jit(solution)/shard_map/ppermute | solution.py:453
  104.8 4.3 %collective-permute-start.10 = (bf16[4,192,128]{2,1,0:T(8,128)(2,1)S(1)}, bf16[4,192,128]{2,1,0:T(8,128)(2,1)S(1)}, u32[]{:S(2)}, u32[]{:S(2)}) collective-permute-start(bf16[4,192,128]{2,1,0:T(8,128)(2,1)S(1)} %get-tuple-element.36), channel_id=1, source_target_pairs={{0,1},{1,2},{2,3},{3,4},{4,5},{5,6},{6,7},{7,8},{8,9},{9,10},{10,1... | collective-permute-start | bytes 589832 | tf_op jit(solution)/shard_map/ppermute | solution.py:392
  109.1 1.3 collective-permute-start.11
  110.4 9.4 %shard_map.124 = (bf16[2,4,192,128]{3,2,1,0:T(8,128)(2,1)}, bf16[16,256,128]{2,1,0:T(8,128)(2,1)S(1)}, bf16[16,256,128]{2,1,0:T(8,128)(2,1)}) custom-call(f32[14]{0:T(128)S(1)} %pad_maximum_fusion.2.table_ref, s32[1]{0:T(128)} %bitcast.6.core_ref, f32[16,8,128]{2,1,0:T(8,128)S(1)} %all-to-all-done.1.parts_ref, ...), custom_call_target="tpu_custom_call" | custom-call | flops 4076863488 | bytes 4484156 | tf_op jit(solution)/shard_map/pallas_call | solution.py:36
  120.8 3.0 %shard_map.131.upstream_ref = f32[2,4,192,128]{3,2,1,0:T(8,128)S(1)} custom-call(f32[14]{0:T(128)S(1)} %pad_maximum_fusion.2.table_ref, bf16[2,4,192,128]{3,2,1,0:T(8,128)(2,1)S(1)} %shard_map.128.refs_0_.own_ref.grad_ref, bf16[2,4,192,128]{3,2,1,0:T(8,128)(2,1)S(1)} %collective-permute-done.9.refs_1_.next_ref, ...), custom_call_target="tpu_custom_call" | custom-call | flops 2038431744 | bytes 3170360 | tf_op jit(solution)/shard_map/pallas_call | solution.py:36
  123.8 1.9 shard_map.132
  127.5 8.3 %all-to-all-start.3 = ((f32[16,8,128]{2,1,0:T(8,128)}), f32[16,8,128]{2,1,0:T(8,128)S(1)}, u32[]{:S(2)}, u32[]{:S(2)}) async-start(f32[16,8,128]{2,1,0:T(8,128)} %get-tuple-element.38), calls=%async_computation.3 | async-start | bytes 131072 | tf_op jit(solution)/shard_map/all_to_all | solution.py:396
  135.8 2.4 %shard_map.135 = bf16[16,256,128]{2,1,0:T(8,128)(2,1)} custom-call(bf16[16,256,128]{2,1,0:T(8,128)(2,1)S(1)} %get-tuple-element.42.kept_ref, bf16[16,256,128]{2,1,0:T(8,128)(2,1)} %collective-permute-done.12.came_ref), custom_call_target="tpu_custom_call" | custom-call | bytes 2097152 | tf_op jit(solution)/shard_map/pallas_call | solution.py:36
  138.3 4.1 %all-to-all-done.3.sums_ref = f32[16,8,128]{2,1,0:T(8,128)S(1)} async-done(((f32[16,8,128]{2,1,0:T(8,128)}), f32[16,8,128]{2,1,0:T(8,128)S(1)}, u32[]{:S(2)}, u32[]{:S(2)}) %all-to-all-start.3) | async-done | bytes 65568 | tf_op jit(solution)/shard_map/all_to_all | solution.py:396
  142.4 3.7 %all-to-all-start.4 = ((bf16[16,256,128]{2,1,0:T(8,128)(2,1)}), bf16[16,256,128]{2,1,0:T(8,128)(2,1)S(1)}, u32[]{:S(2)}, u32[]{:S(2)}) async-start(bf16[16,256,128]{2,1,0:T(8,128)(2,1)} %shard_map.135), calls=%async_computation.4 | async-start | bytes 2097152 | tf_op jit(solution)/shard_map/all_to_all | solution.py:396
  146.1 2.5 %shard_map.138 = bf16[16,256,128]{2,1,0:T(8,128)(2,1)} custom-call(bf16[16,256,128]{2,1,0:T(8,128)(2,1)S(1)} %copy-done.9, bf16[16,256,128]{2,1,0:T(8,128)(2,1)} %collective-permute-done.13.came_ref), custom_call_target="tpu_custom_call" | custom-call | bytes 2097152 | tf_op jit(solution)/shard_map/pallas_call | solution.py:36
  148.6 12.4 %all-to-all-done.4.parts_ref = bf16[16,256,128]{2,1,0:T(8,128)(2,1)S(1)} async-done(((bf16[16,256,128]{2,1,0:T(8,128)(2,1)}), bf16[16,256,128]{2,1,0:T(8,128)(2,1)S(1)}, u32[]{:S(2)}, u32[]{:S(2)}) %all-to-all-start.4) | async-done | bytes 1048608 | tf_op jit(solution)/shard_map/all_to_all | solution.py:396
  161.0 4.2 %all-to-all-start.6 = ((bf16[16,256,128]{2,1,0:T(8,128)(2,1)}), bf16[16,256,128]{2,1,0:T(8,128)(2,1)S(1)}, u32[]{:S(2)}, u32[]{:S(2)}) async-start(bf16[16,256,128]{2,1,0:T(8,128)(2,1)} %shard_map.138), calls=%async_computation.6 | async-start | bytes 2097152 | tf_op jit(solution)/shard_map/all_to_all | solution.py:396
  166.2 13.7 %all-to-all-done.6.parts_ref = bf16[16,256,128]{2,1,0:T(8,128)(2,1)S(1)} async-done(((bf16[16,256,128]{2,1,0:T(8,128)(2,1)}), bf16[16,256,128]{2,1,0:T(8,128)(2,1)S(1)}, u32[]{:S(2)}, u32[]{:S(2)}) %all-to-all-start.6) | async-done | bytes 1048608 | tf_op jit(solution)/shard_map/all_to_all | solution.py:396
  179.9 8.1 %all-to-all-start.5 = ((bf16[8,256,128]{2,1,0:T(8,128)(2,1)}), bf16[8,256,128]{2,1,0:T(8,128)(2,1)S(1)}, u32[]{:S(2)}, u32[]{:S(2)}) async-start(bf16[8,256,128]{2,1,0:T(8,128)(2,1)} %shard_map.136), calls=%async_computation.5 | async-start | bytes 1048576 | tf_op jit(solution)/shard_map/all_to_all | solution.py:512
  188.9 8.5 %all-to-all-done.5.parts_ref = bf16[8,256,128]{2,1,0:T(8,128)(2,1)S(1)} async-done(((bf16[8,256,128]{2,1,0:T(8,128)(2,1)}), bf16[8,256,128]{2,1,0:T(8,128)(2,1)S(1)}, u32[]{:S(2)}, u32[]{:S(2)}) %all-to-all-start.5) | async-done | bytes 524320 | tf_op jit(solution)/shard_map/all_to_all | solution.py:512
  197.4 4.3 %all-to-all-start.7 = ((bf16[8,256,128]{2,1,0:T(8,128)(2,1)}), bf16[8,256,128]{2,1,0:T(8,128)(2,1)S(1)}, u32[]{:S(2)}, u32[]{:S(2)}) async-start(bf16[8,256,128]{2,1,0:T(8,128)(2,1)} %shard_map.139), calls=%async_computation.7 | async-start | bytes 1048576 | tf_op jit(solution)/shard_map/all_to_all | solution.py:512
  201.7 1.1 copy-done.11
  202.8 1.1 copy-done.13
  203.9 1.3 shard_map.133
  206.2 4.9 %all-to-all-done.7.parts_ref = bf16[8,256,128]{2,1,0:T(8,128)(2,1)S(1)} async-done(((bf16[8,256,128]{2,1,0:T(8,128)(2,1)}), bf16[8,256,128]{2,1,0:T(8,128)(2,1)S(1)}, u32[]{:S(2)}, u32[]{:S(2)}) %all-to-all-start.7) | async-done | bytes 524320 | tf_op jit(solution)/shard_map/all_to_all | solution.py:512
  (97 shorter events, 24.1 us)
Async XLA Ops:
  0.6 18.2 %collective-permute-start.1 = (bf16[2,4,192,128]{3,2,1,0:T(8,128)(2,1)}, bf16[2,4,192,128]{3,2,1,0:T(8,128)(2,1)S(1)}, u32[]{:S(2)}, u32[]{:S(2)}) collective-permute-start(bf16[2,4,192,128]{3,2,1,0:T(8,128)(2,1)} %field_ref.1), channel_id=1, source_target_pairs={{0,16},{16,32},{32,48},{48,64},{64,80},{80,96},{96,112},{1,17},{17... | collective-permute-start | bytes 1179656 | tf_op jit(solution)/shard_map/ppermute | solution.py:429
  5.2 13.7 %collective-permute-start.2 = (bf16[2,4,192,128]{3,2,1,0:T(8,128)(2,1)}, bf16[2,4,192,128]{3,2,1,0:T(8,128)(2,1)S(1)}, u32[]{:S(2)}, u32[]{:S(2)}) collective-permute-start(bf16[2,4,192,128]{3,2,1,0:T(8,128)(2,1)} %cot_ref.3), channel_id=1, source_target_pairs={{16,0},{32,16},{48,32},{64,48},{80,64},{96,80},{112,96},{17,1},{33... | collective-permute-start | bytes 1179656 | tf_op jit(solution)/shard_map/ppermute | solution.py:430
  7.1 1.0 copy-start
  8.1 18.7 %copy-start.30 = (f32[192]{0:T(256)S(1)}, f32[192]{0:T(256)}, u32[]{:S(2)}) copy-start(f32[192]{0:T(256)} %param.15) | copy-start | bytes 2308
  8.1 18.7 %copy-start.31 = (f32[192]{0:T(256)S(1)}, f32[192]{0:T(256)}, u32[]{:S(2)}) copy-start(f32[192]{0:T(256)} %param.14) | copy-start | bytes 2308
  8.1 18.7 %copy-start.32 = (f32[192]{0:T(256)S(1)}, f32[192]{0:T(256)}, u32[]{:S(2)}) copy-start(f32[192]{0:T(256)} %param.13) | copy-start | bytes 2308
  8.1 18.7 %copy-start.33 = (f32[192]{0:T(256)S(1)}, f32[192]{0:T(256)}, u32[]{:S(2)}) copy-start(f32[192]{0:T(256)} %param.12) | copy-start | bytes 2308
  10.0 19.7 %all-to-all-start = ((f32[16,8,128]{2,1,0:T(8,128)}), f32[16,8,128]{2,1,0:T(8,128)S(1)}, u32[]{:S(2)}, u32[]{:S(2)}) async-start(f32[16,8,128]{2,1,0:T(8,128)} %shard_map.120), calls=%async_computation | async-start | bytes 131072 | tf_op jit(solution)/shard_map/all_to_all | solution.py:396
  18.9 8.1 %copy-start.21 = (bf16[2,4,192,128]{3,2,1,0:T(8,128)(2,1)}, bf16[2,4,192,128]{3,2,1,0:T(8,128)(2,1)S(1)}, u32[]{:S(2)}) copy-start(bf16[2,4,192,128]{3,2,1,0:T(8,128)(2,1)S(1)} %collective-permute-done.1.refs_0_.prev_ref) | copy-start | bytes 1179652
  18.9 1.1 copy-start.1
  20.0 1.0 copy-start.6
  21.0 5.8 %copy-start.19 = (bf16[2,4,192,128]{3,2,1,0:T(8,128)(2,1)}, bf16[2,4,192,128]{3,2,1,0:T(8,128)(2,1)S(1)}, u32[]{:S(2)}) copy-start(bf16[2,4,192,128]{3,2,1,0:T(8,128)(2,1)S(1)} %collective-permute-done.2.refs_3_.next_ref) | copy-start | bytes 1179652
  22.0 13.4 %collective-permute-start.3 = (bf16[8,192,128]{2,1,0:T(8,128)(2,1)}, bf16[8,192,128]{2,1,0:T(8,128)(2,1)S(1)}, u32[]{:S(2)}, u32[]{:S(2)}) collective-permute-start(bf16[8,192,128]{2,1,0:T(8,128)(2,1)} %get-tuple-element.25), channel_id=1, source_target_pairs={{0,1},{1,2},{2,3},{3,4},{4,5},{5,6},{6,7},{7,8},{8,9},{9,10},{10,1... | collective-permute-start | bytes 1179656 | tf_op jit(solution)/shard_map/ppermute | solution.py:392
  25.3 12.4 %collective-permute-start.4 = (bf16[8,192,128]{2,1,0:T(8,128)(2,1)}, bf16[8,192,128]{2,1,0:T(8,128)(2,1)S(1)}, u32[]{:S(2)}, u32[]{:S(2)}) collective-permute-start(bf16[8,192,128]{2,1,0:T(8,128)(2,1)} %get-tuple-element.26), channel_id=1, source_target_pairs={{1,0},{2,1},{3,2},{4,3},{5,4},{6,5},{7,6},{8,7},{9,8},{10,9},{11,1... | collective-permute-start | bytes 1179656 | tf_op jit(solution)/shard_map/ppermute | solution.py:392
  27.0 11.5 %copy-start.2 = (bf16[2,4,192,128]{3,2,1,0:T(8,128)(2,1)S(1)}, bf16[2,4,192,128]{3,2,1,0:T(8,128)(2,1)}, u32[]{:S(2)}) copy-start(bf16[2,4,192,128]{3,2,1,0:T(8,128)(2,1)} %field_ref.1) | copy-start | bytes 1179652
  27.0 1.6 copy-start.5
  29.7 5.8 %collective-permute-start = (f32[16,8,128]{2,1,0:T(8,128)S(1)}, f32[16,8,128]{2,1,0:T(8,128)S(1)}, u32[]{:S(2)}, u32[]{:S(2)}) collective-permute-start(f32[16,8,128]{2,1,0:T(8,128)S(1)} %all-to-all-done.parts_ref), channel_id=1, source_target_pairs={{0,16},{16,32},{32,48},{48,64},{64,80},{80,96},{96,112},{1,17},{17... | collective-permute-start | bytes 196616 | tf_op jit(solution)/shard_map/ppermute | solution.py:433
  38.4 1.6 copy-start.3
  41.0 1.0 copy-start.24
  42.0 1.0 copy-start.27
  43.0 15.9 %copy-start.7 = (bf16[2,4,192,128]{3,2,1,0:T(8,128)(2,1)S(1)}, bf16[2,4,192,128]{3,2,1,0:T(8,128)(2,1)}, u32[]{:S(2)}) copy-start(bf16[2,4,192,128]{3,2,1,0:T(8,128)(2,1)} %cot_ref.3) | copy-start | bytes 1179652
  50.9 14.9 %all-to-all-start.1 = ((f32[16,8,128]{2,1,0:T(8,128)}), f32[16,8,128]{2,1,0:T(8,128)S(1)}, u32[]{:S(2)}, u32[]{:S(2)}) async-start(f32[16,8,128]{2,1,0:T(8,128)} %get-tuple-element.27), calls=%async_computation.1 | async-start | bytes 131072 | tf_op jit(solution)/shard_map/all_to_all | solution.py:396
  58.9 1.0 copy-start.20
  60.9 1.0 copy-start.28
  65.8 1.1 copy-start.15
  66.9 1.1 copy-start.18
  70.0 13.2 %all-to-all-start.2 = ((f32[16,8,128]{2,1,0:T(8,128)}), f32[16,8,128]{2,1,0:T(8,128)S(1)}, u32[]{:S(2)}, u32[]{:S(2)}) async-start(f32[16,8,128]{2,1,0:T(8,128)} %get-tuple-element.33), calls=%async_computation.2 | async-start | bytes 131072 | tf_op jit(solution)/shard_map/all_to_all | solution.py:396
  76.6 18.0 %collective-permute-start.6 = (bf16[2,4,192,128]{3,2,1,0:T(8,128)(2,1)S(1)}, bf16[2,4,192,128]{3,2,1,0:T(8,128)(2,1)}, u32[]{:S(2)}, u32[]{:S(2)}) collective-permute-start(bf16[2,4,192,128]{3,2,1,0:T(8,128)(2,1)S(1)} %get-tuple-element.29.refs_1_), channel_id=1, source_target_pairs={{0,16},{16,32},{32,48},{48,64},{64,80},{80,96},{96,112},{1,17},{17... | collective-permute-start | bytes 1179656 | tf_op jit(solution)/shard_map/ppermute | solution.py:443
  83.7 2.0 copy-start.29
  85.7 18.0 %copy-start.4 = (bf16[5184,192]{0,1:T(8,128)(2,1)S(1)}, bf16[5184,192]{0,1:T(8,128)(2,1)}, u32[]{:S(2)}) copy-start(bf16[5184,192]{0,1:T(8,128)(2,1)} %param.10) | copy-start | bytes 5971972
  90.6 45.2 %collective-permute-start.12 = (bf16[16,256,128]{2,1,0:T(8,128)(2,1)}, bf16[16,256,128]{2,1,0:T(8,128)(2,1)}, u32[]{:S(2)}, u32[]{:S(2)}) collective-permute-start(bf16[16,256,128]{2,1,0:T(8,128)(2,1)} %get-tuple-element.43), channel_id=1, source_target_pairs={{0,16},{16,0},{32,48},{48,32},{64,80},{80,64},{96,112},{112,96},{1... | collective-permute-start | bytes 3145736 | tf_op jit(solution)/shard_map/ppermute | solution.py:507
  92.7 12.0 %collective-permute-start.9 = (bf16[2,4,192,128]{3,2,1,0:T(8,128)(2,1)S(1)}, bf16[2,4,192,128]{3,2,1,0:T(8,128)(2,1)S(1)}, u32[]{:S(2)}, u32[]{:S(2)}) collective-permute-start(bf16[2,4,192,128]{3,2,1,0:T(8,128)(2,1)S(1)} %shard_map.128.refs_0_.own_ref.grad_ref), channel_id=1, source_target_pairs={{16,0},{32,16},{48,32},{64,48},{80,64},{96,80},{112,96},{17,1},{33... | collective-permute-start | bytes 1179656 | tf_op jit(solution)/shard_map/ppermute | solution.py:476
  95.7 14.7 %collective-permute-start.7 = (bf16[4,192,128]{2,1,0:T(8,128)(2,1)S(1)}, bf16[4,192,128]{2,1,0:T(8,128)(2,1)S(1)}, u32[]{:S(2)}, u32[]{:S(2)}) collective-permute-start(bf16[4,192,128]{2,1,0:T(8,128)(2,1)S(1)} %get-tuple-element.30), channel_id=1, source_target_pairs={{0,1},{1,2},{2,3},{3,4},{4,5},{5,6},{6,7},{7,8},{8,9},{9,10},{10,1... | collective-permute-start | bytes 589832 | tf_op jit(solution)/shard_map/ppermute | solution.py:392
  97.9 12.5 %copy-start.16 = (f32[2,4,192,128]{3,2,1,0:T(8,128)S(1)}, f32[2,4,192,128]{3,2,1,0:T(8,128)}, u32[]{:S(2)}) copy-start(f32[2,4,192,128]{3,2,1,0:T(8,128)} %copy-done.14) | copy-start | bytes 2359300
  97.9 12.5 %collective-permute-start.8 = (bf16[4,192,128]{2,1,0:T(8,128)(2,1)S(1)}, bf16[4,192,128]{2,1,0:T(8,128)(2,1)S(1)}, u32[]{:S(2)}, u32[]{:S(2)}) collective-permute-start(bf16[4,192,128]{2,1,0:T(8,128)(2,1)S(1)} %get-tuple-element.31), channel_id=1, source_target_pairs={{1,0},{2,1},{3,2},{4,3},{5,4},{6,5},{7,6},{8,7},{9,8},{10,9},{11,1... | collective-permute-start | bytes 589832 | tf_op jit(solution)/shard_map/ppermute | solution.py:392
  99.3 9.7 %collective-permute-start.5 = (f32[16,8,128]{2,1,0:T(8,128)S(1)}, f32[16,8,128]{2,1,0:T(8,128)S(1)}, u32[]{:S(2)}, u32[]{:S(2)}) collective-permute-start(f32[16,8,128]{2,1,0:T(8,128)S(1)} %all-to-all-done.1.parts_ref), channel_id=1, source_target_pairs={{0,16},{16,32},{32,48},{48,64},{64,80},{80,96},{96,112},{1,17},{17... | collective-permute-start | bytes 196616 | tf_op jit(solution)/shard_map/ppermute | solution.py:453
  104.8 16.0 %collective-permute-start.10 = (bf16[4,192,128]{2,1,0:T(8,128)(2,1)S(1)}, bf16[4,192,128]{2,1,0:T(8,128)(2,1)S(1)}, u32[]{:S(2)}, u32[]{:S(2)}) collective-permute-start(bf16[4,192,128]{2,1,0:T(8,128)(2,1)S(1)} %get-tuple-element.36), channel_id=1, source_target_pairs={{0,1},{1,2},{2,3},{3,4},{4,5},{5,6},{6,7},{7,8},{8,9},{9,10},{10,1... | collective-permute-start | bytes 589832 | tf_op jit(solution)/shard_map/ppermute | solution.py:392
  109.1 11.7 %collective-permute-start.11 = (bf16[4,192,128]{2,1,0:T(8,128)(2,1)S(1)}, bf16[4,192,128]{2,1,0:T(8,128)(2,1)S(1)}, u32[]{:S(2)}, u32[]{:S(2)}) collective-permute-start(bf16[4,192,128]{2,1,0:T(8,128)(2,1)S(1)} %get-tuple-element.37), channel_id=1, source_target_pairs={{1,0},{2,1},{3,2},{4,3},{5,4},{6,5},{7,6},{8,7},{9,8},{10,9},{11,1... | collective-permute-start | bytes 589832 | tf_op jit(solution)/shard_map/ppermute | solution.py:392
  119.7 1.0 copy-start.8
  120.8 25.3 %collective-permute-start.13 = (bf16[16,256,128]{2,1,0:T(8,128)(2,1)}, bf16[16,256,128]{2,1,0:T(8,128)(2,1)}, u32[]{:S(2)}, u32[]{:S(2)}) collective-permute-start(bf16[16,256,128]{2,1,0:T(8,128)(2,1)} %get-tuple-element.45), channel_id=1, source_target_pairs={{0,16},{16,0},{32,48},{48,32},{64,80},{80,64},{96,112},{112,96},{1... | collective-permute-start | bytes 3145736 | tf_op jit(solution)/shard_map/ppermute | solution.py:507
  127.5 14.9 %all-to-all-start.3 = ((f32[16,8,128]{2,1,0:T(8,128)}), f32[16,8,128]{2,1,0:T(8,128)S(1)}, u32[]{:S(2)}, u32[]{:S(2)}) async-start(f32[16,8,128]{2,1,0:T(8,128)} %get-tuple-element.38), calls=%async_computation.3 | async-start | bytes 131072 | tf_op jit(solution)/shard_map/all_to_all | solution.py:396
  138.3 7.8 %copy-start.9 = (bf16[16,256,128]{2,1,0:T(8,128)(2,1)S(1)}, bf16[16,256,128]{2,1,0:T(8,128)(2,1)}, u32[]{:S(2)}) copy-start(bf16[16,256,128]{2,1,0:T(8,128)(2,1)} %copy-done.8) | copy-start | bytes 3145732
  142.4 18.6 %all-to-all-start.4 = ((bf16[16,256,128]{2,1,0:T(8,128)(2,1)}), bf16[16,256,128]{2,1,0:T(8,128)(2,1)S(1)}, u32[]{:S(2)}, u32[]{:S(2)}) async-start(bf16[16,256,128]{2,1,0:T(8,128)(2,1)} %shard_map.135), calls=%async_computation.4 | async-start | bytes 2097152 | tf_op jit(solution)/shard_map/all_to_all | solution.py:396
  161.0 18.9 %all-to-all-start.6 = ((bf16[16,256,128]{2,1,0:T(8,128)(2,1)}), bf16[16,256,128]{2,1,0:T(8,128)(2,1)S(1)}, u32[]{:S(2)}, u32[]{:S(2)}) async-start(bf16[16,256,128]{2,1,0:T(8,128)(2,1)} %shard_map.138), calls=%async_computation.6 | async-start | bytes 2097152 | tf_op jit(solution)/shard_map/all_to_all | solution.py:396
  179.9 17.5 %all-to-all-start.5 = ((bf16[8,256,128]{2,1,0:T(8,128)(2,1)}), bf16[8,256,128]{2,1,0:T(8,128)(2,1)S(1)}, u32[]{:S(2)}, u32[]{:S(2)}) async-start(bf16[8,256,128]{2,1,0:T(8,128)(2,1)} %shard_map.136), calls=%async_computation.5 | async-start | bytes 1048576 | tf_op jit(solution)/shard_map/all_to_all | solution.py:512
  197.4 13.8 %all-to-all-start.7 = ((bf16[8,256,128]{2,1,0:T(8,128)(2,1)}), bf16[8,256,128]{2,1,0:T(8,128)(2,1)S(1)}, u32[]{:S(2)}, u32[]{:S(2)}) async-start(bf16[8,256,128]{2,1,0:T(8,128)(2,1)} %shard_map.139), calls=%async_computation.7 | async-start | bytes 1048576 | tf_op jit(solution)/shard_map/all_to_all | solution.py:512
  201.7 1.1 copy-start.11
  202.8 1.1 copy-start.13
  (8 other events, 7.0 us)
